TPU v7x, 512 devices: a whole 4x4x16 slice. The times are simulated.
512 devices in a mesh: req: 32 (over y, z_lo), tp: 16 (over x, z_hi, core).
Axes of the slice: x: 4, y: 4, z: 16 (z_hi: 2, z_lo: 8; z = z_hi * 8 + z_lo), core: 2. Of those that a mesh axis runs over, the one named last changes fastest.
Arguments:
- state: float32 [384, 32, 128, 128], P('req', 'tp'), may hold values from -4 to 4
- conv_state: float32 [384, 16, 3, 512], P('req', 'tp'), may hold values from -6 to 6
- mixed: bfloat16 [384, 4, 16, 512], P('req', None, 'tp'), may hold values from -6 to 6
- gates: float32 [384, 4, 2, 32], P('req', None, None, 'tp'), may hold values from -6 to 6
- output_gate: bfloat16 [384, 4, 4096], P('req', None, 'tp'), may hold values from -6 to 6
- conv_weight: float32 [16, 4, 512], P('tp'), may hold values from -3 to 3
- decay_log: float32 [32], P('tp'), may hold values from -1.5 to 1.5
- time_bias: float32 [32], P('tp'), may hold values from -2 to 1
- norm_gain: float32 [128], replicated, may hold values from 0.25 to 1.75
- out_weight: bfloat16 [4096, 2048], P('tp'), may hold values from -0.09375 to 0.09375
- partner: int32 [32, 3], replicated, may hold values from 0 to 31, as said below
- moved_slots: int32 [32, 3], P('req'), may hold values from 0 to 11, as said below
Outputs:
- hidden_out: bfloat16 [384, 4, 2048], P('req')
- new_state: float32 [384, 32, 128, 128], P('req', 'tp')
- new_conv_state: float32 [384, 16, 3, 512], P('req', 'tp')
Inputs may be any that keep to these rules, and one draw needn't show every extreme that they name: partner[g, j] = g XOR m_j, where each m_j lies in 1 to 31 and is common to all groups. `moved_slots`: each row holds 3 different slots.
All inputs are finite; a program needn't handle non-finite values.
Results may differ from a plain program's by a relative error of at most 0.0075.
Values may be sent and summed in bfloat16 or wider, within the bound.
A program may use at most 128 MiB of HBM per device.

v0:
```python
import jax
import jax.numpy as jnp
from jax import lax
from jax.sharding import PartitionSpec as P


def swapped(block, axis, apart):
    count = lax.axis_size(axis)
    route = []
    for low in range(count):
        high = low | 1 << apart
        if high != low and high < count:
            route += [(low, high), (high, low)]
    return lax.ppermute(block, axis, route)


def advance(
    state, conv_state, mixed, gates, output_gate, conv_weight, decay_log, time_bias, norm_gain
):
    rows = mixed.shape[0]
    width = mixed.shape[3] // 4
    value_heads = state.shape[1]
    scale_a = jnp.exp(decay_log)
    gathered = []
    for step in range(mixed.shape[1]):
        latest = mixed[:, step].astype(jnp.float32)
        window = jnp.concatenate([conv_state, latest[:, :, None, :]], axis=2)
        conv = jax.nn.silu(jnp.sum(window * conv_weight[None], axis=2))
        conv_state = window[:, :, 1:]
        query = conv[..., :width]
        keyvec = conv[..., width : 2 * width]
        values = conv[..., 2 * width :].reshape(rows, value_heads, -1)
        query = (
            query
            * lax.rsqrt(jnp.sum(query * query, -1, keepdims=True) + 1e-06)
            / jnp.sqrt(jnp.float32(width))
        )
        keyvec = keyvec * lax.rsqrt(jnp.sum(keyvec * keyvec, -1, keepdims=True) + 1e-06)
        query = jnp.repeat(query, 2, axis=1)
        keyvec = jnp.repeat(keyvec, 2, axis=1)
        decay = jnp.exp(-scale_a * jax.nn.softplus(gates[:, step, 0] + time_bias))
        beta = jax.nn.sigmoid(gates[:, step, 1])
        state = state * decay[..., None, None]
        readout = jnp.einsum("nhk,nhkv->nhv", keyvec, state, precision=lax.Precision.HIGHEST)
        delta = (values - readout) * beta[..., None]
        state = state + keyvec[..., :, None] * delta[..., None, :]
        result = jnp.einsum("nhk,nhkv->nhv", query, state, precision=lax.Precision.HIGHEST)
        zvalue = output_gate[:, step].astype(jnp.float32).reshape(rows, value_heads, -1)
        normed = result * lax.rsqrt(jnp.mean(result * result, -1, keepdims=True) + 1e-06)
        gated = (normed * norm_gain * jax.nn.silu(zvalue)).astype(jnp.bfloat16)
        gathered.append(gated.reshape(rows, -1))
    return (jnp.stack(gathered, axis=1), state, conv_state)


def route_block(packed, partner):
    group = lax.axis_index("req")
    offsets = jnp.bitwise_xor(partner[group], group)
    current = packed
    for bit_pos in range(lax.axis_size("req").bit_length() - 1):
        taken_rows = jnp.bitwise_and(jnp.right_shift(offsets, bit_pos), 1) == 1
        needed = jnp.any(taken_rows)

        def moved(block, bit_pos=bit_pos):
            return swapped(block.astype(jnp.bfloat16), "req", bit_pos).astype(block.dtype)

        def stayed(block):
            return block

        arrived = lax.cond(needed, moved, stayed, current)
        current = jnp.where(taken_rows[:, None], arrived, current)
    return current


def per_device(
    state,
    conv_state,
    mixed,
    gates,
    output_gate,
    conv_weight,
    decay_log,
    time_bias,
    norm_gain,
    out_weight,
    partner,
    moved_slots,
):
    slots = moved_slots[0]
    count = slots.shape[0]
    state_size = state[0].size
    outgoing = jnp.concatenate(
        [state[slots].reshape(count, -1), conv_state[slots].reshape(count, -1)], axis=1
    )
    params = (conv_weight, decay_log, time_bias, norm_gain)
    incoming = route_block(outgoing, partner)
    start_state = state.at[slots].set(incoming[:, :state_size].reshape((count,) + state.shape[1:]))
    start_conv = conv_state.at[slots].set(
        incoming[:, state_size:].reshape((count,) + conv_state.shape[1:])
    )
    gated, final_state, final_conv = advance(
        start_state, start_conv, mixed, gates, output_gate, *params
    )
    flat = gated.reshape(-1, gated.shape[-1])
    terms = jnp.dot(flat, out_weight, preferred_element_type=jnp.float32).reshape(
        gated.shape[0], gated.shape[1], -1
    )
    hidden_out = lax.psum(terms, "tp").astype(jnp.bfloat16)
    return (hidden_out, final_state, final_conv)


def solution(mesh):
    placed = (
        P("req", "tp", None, None),
        P("req", "tp", None, None),
        P("req", None, "tp", None),
        P("req", None, None, "tp"),
        P("req", None, "tp"),
        P("tp", None, None),
        P("tp"),
        P("tp"),
        P(),
        P("tp", None),
        P(),
        P("req", None),
    )
    return jax.shard_map(
        per_device,
        mesh=mesh,
        in_specs=placed,
        out_specs=(P("req", None, None), P("req", "tp", None, None), P("req", "tp", None, None)),
        check_vma=False,
    )
```

profile of v0, /device:TPU:24, one launch (start us, length us, event | category | flops | bytes accessed | tf_op | source)
XLA Modules:
  0.0 270.0 jit_solution(9499823360947720110)
XLA Ops:
  0.7 1.5 copy.72
  2.5 0.7 fusion.74
  4.5 0.7 fusion.76
  6.4 0.7 fusion.78
  7.8 1.3 gather_fusion
  9.1 1.3 bitcast_dynamic-update-slice_fusion
  10.4 0.6 gather_fusion.1
  11.0 11.4 %conditional.5 = (f32[3,34304]{1,0:T(4,128)}) conditional(s32[]{:T(128)} %convert_element_type.116, f32[3,34304]{1,0:T(4,128)S(1)} %constant_dynamic-update-slice_fusion, f32[3,34304]{1,0:T(4,128)S(1)} %constant_dynamic-update-slice_fusion), branch_computations={%region_5.6_spmd, %region_6.7_spmd} | conditional | flops 205824 | bytes 2058288 | solution.py:69
  11.0 0.1 convert_element_type.80
  11.1 3.8 %collective-permute-start = (bf16[3,34304]{1,0:T(4,128)(2,1)S(1)}, bf16[3,34304]{1,0:T(4,128)(2,1)S(1)}, u32[]{:S(2)}, u32[]{:S(2)}) collective-permute-start(bf16[3,34304]{1,0:T(4,128)(2,1)S(1)} %convert_element_type.80), channel_id=1, source_target_pairs={{0,16},{16,0},{32,48},{48,32},{64,80},{80,64},{96,112},{112,96},{1... | collective-permute-start | bytes 617480 | tf_op jit(solution)/shard_map/cond/branch_1_fun/ppermute | solution.py:14
  14.9 6.6 %collective-permute-done = bf16[3,34304]{1,0:T(4,128)(2,1)S(1)} collective-permute-done((bf16[3,34304]{1,0:T(4,128)(2,1)S(1)}, bf16[3,34304]{1,0:T(4,128)(2,1)S(1)}, u32[]{:S(2)}, u32[]{:S(2)}) %collective-permute-start) | collective-permute-done | bytes 205856 | tf_op jit(solution)/shard_map/cond/branch_1_fun/ppermute | solution.py:14
  21.5 0.9 convert_element_type.81
  22.3 2.1 broadcast_select_fusion
  24.4 18.2 %conditional.6 = (f32[3,34304]{1,0:T(4,128)S(1)}) conditional(s32[]{:T(128)} %convert_element_type.115, f32[3,34304]{1,0:T(4,128)} %broadcast_select_fusion, f32[3,34304]{1,0:T(4,128)} %broadcast_select_fusion), branch_computations={%region_7.8_spmd, %region_8.9_spmd} | conditional | flops 205824 | bytes 2058288 | solution.py:69
  24.4 1.1 convert_element_type.82
  25.5 5.2 %collective-permute-start.1 = (bf16[3,34304]{1,0:T(4,128)(2,1)S(1)}, bf16[3,34304]{1,0:T(4,128)(2,1)S(1)}, u32[]{:S(2)}, u32[]{:S(2)}) collective-permute-start(bf16[3,34304]{1,0:T(4,128)(2,1)S(1)} %convert_element_type.82), channel_id=1, source_target_pairs={{0,32},{32,0},{16,48},{48,16},{64,96},{96,64},{80,112},{112,80},{1... | collective-permute-start | bytes 617480 | tf_op jit(solution)/shard_map/cond/branch_1_fun/ppermute | solution.py:14
  30.7 11.8 %collective-permute-done.1 = bf16[3,34304]{1,0:T(4,128)(2,1)S(1)} collective-permute-done((bf16[3,34304]{1,0:T(4,128)(2,1)S(1)}, bf16[3,34304]{1,0:T(4,128)(2,1)S(1)}, u32[]{:S(2)}, u32[]{:S(2)}) %collective-permute-start.1) | collective-permute-done | bytes 205856 | tf_op jit(solution)/shard_map/cond/branch_1_fun/ppermute | solution.py:14
  42.6 0.8 copy-done.5
  43.4 1.4 broadcast_select_fusion.1
  44.8 32.4 %conditional.7 = (f32[3,34304]{1,0:T(4,128)}) conditional(s32[]{:T(128)} %convert_element_type.114, f32[3,34304]{1,0:T(4,128)S(1)} %broadcast_select_fusion.1, f32[3,34304]{1,0:T(4,128)S(1)} %broadcast_select_fusion.1), branch_computations={%region_9.10_spmd, %region_10.11_spmd} | conditional | flops 205824 | bytes 2058288 | solution.py:69
  44.8 0.1 convert_element_type.84
  44.9 9.1 %collective-permute-start.2 = (bf16[3,34304]{1,0:T(4,128)(2,1)S(1)}, bf16[3,34304]{1,0:T(4,128)(2,1)S(1)}, u32[]{:S(2)}, u32[]{:S(2)}) collective-permute-start(bf16[3,34304]{1,0:T(4,128)(2,1)S(1)} %convert_element_type.84), channel_id=1, source_target_pairs={{0,64},{64,0},{16,80},{80,16},{32,96},{96,32},{48,112},{112,48},{1... | collective-permute-start | bytes 617480 | tf_op jit(solution)/shard_map/cond/branch_1_fun/ppermute | solution.py:14
  54.0 22.3 %collective-permute-done.2 = bf16[3,34304]{1,0:T(4,128)(2,1)S(1)} collective-permute-done((bf16[3,34304]{1,0:T(4,128)(2,1)S(1)}, bf16[3,34304]{1,0:T(4,128)(2,1)S(1)}, u32[]{:S(2)}, u32[]{:S(2)}) %collective-permute-start.2) | collective-permute-done | bytes 205856 | tf_op jit(solution)/shard_map/cond/branch_1_fun/ppermute | solution.py:14
  76.3 0.9 convert_element_type.85
  77.2 1.3 broadcast_select_fusion.2
  78.5 0.8 copy-done.1
  79.3 10.5 %conditional.8 = (f32[3,34304]{1,0:T(4,128)S(1)}) conditional(s32[]{:T(128)} %convert_element_type.113, f32[3,34304]{1,0:T(4,128)S(1)} %broadcast_select_fusion.2, f32[3,34304]{1,0:T(4,128)S(1)} %broadcast_select_fusion.2), branch_computations={%region_11.12_spmd, %region_12.13_spmd} | conditional | flops 205824 | bytes 2058288 | solution.py:69
  79.3 0.1 convert_element_type.86
  79.4 2.7 collective-permute-start.3
  82.0 7.7 %collective-permute-done.3 = bf16[3,34304]{1,0:T(4,128)(2,1)S(1)} collective-permute-done((bf16[3,34304]{1,0:T(4,128)(2,1)S(1)}, bf16[3,34304]{1,0:T(4,128)(2,1)S(1)}, u32[]{:S(2)}, u32[]{:S(2)}) %collective-permute-start.3) | collective-permute-done | bytes 205856 | tf_op jit(solution)/shard_map/cond/branch_1_fun/ppermute | solution.py:14
  89.8 0.8 copy-done.6
  90.6 1.4 broadcast_select_fusion.3
  92.0 12.0 %conditional.9 = (f32[3,34304]{1,0:T(4,128)}) conditional(s32[]{:T(128)} %convert_element_type.112, f32[3,34304]{1,0:T(4,128)S(1)} %broadcast_select_fusion.3, f32[3,34304]{1,0:T(4,128)S(1)} %broadcast_select_fusion.3), branch_computations={%region_13.14_spmd, %region_14.15_spmd} | conditional | flops 205824 | bytes 2058288 | solution.py:69
  92.1 0.1 convert_element_type.88
  92.2 3.1 %collective-permute-start.4 = (bf16[3,34304]{1,0:T(4,128)(2,1)S(1)}, bf16[3,34304]{1,0:T(4,128)(2,1)S(1)}, u32[]{:S(2)}, u32[]{:S(2)}) collective-permute-start(bf16[3,34304]{1,0:T(4,128)(2,1)S(1)} %convert_element_type.88), channel_id=1, source_target_pairs={{0,256},{256,0},{16,272},{272,16},{32,288},{288,32},{48,304},{304,... | collective-permute-start | bytes 617480 | tf_op jit(solution)/shard_map/cond/branch_1_fun/ppermute | solution.py:14
  95.3 7.9 %collective-permute-done.4 = bf16[3,34304]{1,0:T(4,128)(2,1)S(1)} collective-permute-done((bf16[3,34304]{1,0:T(4,128)(2,1)S(1)}, bf16[3,34304]{1,0:T(4,128)(2,1)S(1)}, u32[]{:S(2)}, u32[]{:S(2)}) %collective-permute-start.4) | collective-permute-done | bytes 205856 | tf_op jit(solution)/shard_map/cond/branch_1_fun/ppermute | solution.py:14
  103.2 0.9 convert_element_type.89
  104.1 1.3 broadcast_select_fusion.4
  105.3 0.8 copy-done.3
  106.2 0.6 scatter_fusion
  107.1 0.6 fusion.31
  107.7 0.1 multiply_reduce_fusion.11
  108.1 1.0 scatter_fusion.1
  109.3 0.1 copy.24
  109.4 1.5 fusion.6
  110.9 0.1 copy.25
  111.1 1.5 fusion.10
  112.8 0.1 multiply_reduce_fusion.9
  113.1 1.6 fusion.4
  114.9 1.7 fusion.73
  116.7 0.1 multiply_reduce_fusion.7
  117.0 0.1 copy.28
  117.1 1.7 fusion.2
  119.0 1.9 fusion.11
  121.0 0.1 multiply_reduce_fusion.4
  121.4 1.9 fusion
  123.5 1.5 multiply_add_fusion
  125.0 1.1 copy-done.2
  126.2 1.4 fusion.79
  127.7 0.1 fusion.62
  127.9 0.3 fusion.8
  128.2 140.3 %all-reduce.1 = bf16[12,4,2048]{2,0,1:T(8,128)(2,1)S(1)} all-reduce(f32[12,4,2048]{2,0,1:T(8,128)S(1)} %fusion.8), channel_id=1, replica_groups=mesh['req'=32,'tp'=16] {'tp'}, use_global_device_ids=true, to_apply=%region_33.34 | all-reduce | flops 98304 | bytes 589824 | tf_op jit(solution)/shard_map/psum | solution.py:107
  268.5 0.8 copy.32
  269.3 0.7 fusion.32
  (103 shorter events, 2.8 us)
Async XLA Ops:
  0.6 127.3 %copy-start = (bf16[256,2048]{1,0:T(8,128)(2,1)S(1)}, bf16[256,2048]{1,0:T(8,128)(2,1)}, u32[]{:S(2)}) copy-start(bf16[256,2048]{1,0:T(8,128)(2,1)} %param.31) | copy-start | bytes 3145732
  0.6 1.7 copy-start.9
  0.7 1.6 copy-start.7
  0.7 1.5 copy-start.8
  0.7 1.7 copy-start.12
  0.7 1.7 copy-start.15
  11.1 10.4 %collective-permute-start = (bf16[3,34304]{1,0:T(4,128)(2,1)S(1)}, bf16[3,34304]{1,0:T(4,128)(2,1)S(1)}, u32[]{:S(2)}, u32[]{:S(2)}) collective-permute-start(bf16[3,34304]{1,0:T(4,128)(2,1)S(1)} %convert_element_type.80), channel_id=1, source_target_pairs={{0,16},{16,0},{32,48},{48,32},{64,80},{80,64},{96,112},{112,96},{1... | collective-permute-start | bytes 617480 | tf_op jit(solution)/shard_map/cond/branch_1_fun/ppermute | solution.py:14
  25.5 17.0 %collective-permute-start.1 = (bf16[3,34304]{1,0:T(4,128)(2,1)S(1)}, bf16[3,34304]{1,0:T(4,128)(2,1)S(1)}, u32[]{:S(2)}, u32[]{:S(2)}) collective-permute-start(bf16[3,34304]{1,0:T(4,128)(2,1)S(1)} %convert_element_type.82), channel_id=1, source_target_pairs={{0,32},{32,0},{16,48},{48,16},{64,96},{96,64},{80,112},{112,80},{1... | collective-permute-start | bytes 617480 | tf_op jit(solution)/shard_map/cond/branch_1_fun/ppermute | solution.py:14
  42.6 0.8 copy-start.5
  44.9 31.4 %collective-permute-start.2 = (bf16[3,34304]{1,0:T(4,128)(2,1)S(1)}, bf16[3,34304]{1,0:T(4,128)(2,1)S(1)}, u32[]{:S(2)}, u32[]{:S(2)}) collective-permute-start(bf16[3,34304]{1,0:T(4,128)(2,1)S(1)} %convert_element_type.84), channel_id=1, source_target_pairs={{0,64},{64,0},{16,80},{80,16},{32,96},{96,32},{48,112},{112,48},{1... | collective-permute-start | bytes 617480 | tf_op jit(solution)/shard_map/cond/branch_1_fun/ppermute | solution.py:14
  78.5 0.8 copy-start.1
  79.4 10.4 %collective-permute-start.3 = (bf16[3,34304]{1,0:T(4,128)(2,1)S(1)}, bf16[3,34304]{1,0:T(4,128)(2,1)S(1)}, u32[]{:S(2)}, u32[]{:S(2)}) collective-permute-start(bf16[3,34304]{1,0:T(4,128)(2,1)S(1)} %convert_element_type.86), channel_id=1, source_target_pairs={{0,128},{128,0},{16,144},{144,16},{32,160},{160,32},{48,176},{176,... | collective-permute-start | bytes 617480 | tf_op jit(solution)/shard_map/cond/branch_1_fun/ppermute | solution.py:14
  89.8 0.8 copy-start.6
  92.2 11.0 %collective-permute-start.4 = (bf16[3,34304]{1,0:T(4,128)(2,1)S(1)}, bf16[3,34304]{1,0:T(4,128)(2,1)S(1)}, u32[]{:S(2)}, u32[]{:S(2)}) collective-permute-start(bf16[3,34304]{1,0:T(4,128)(2,1)S(1)} %convert_element_type.88), channel_id=1, source_target_pairs={{0,256},{256,0},{16,272},{272,16},{32,288},{288,32},{48,304},{304,... | collective-permute-start | bytes 617480 | tf_op jit(solution)/shard_map/cond/branch_1_fun/ppermute | solution.py:14
  104.1 3.0 %copy-start.10 = (f32[1,4,512]{2,1,0:T(4,128)S(1)}, f32[1,4,512]{2,1,0:T(4,128)}, u32[]{:S(2)}) copy-start(f32[1,4,512]{2,1,0:T(4,128)} %param.27) | copy-start | bytes 24580
  105.3 0.8 copy-start.3
  106.1 1.8 copy-start.4
  108.0 1.2 copy-start.16
  108.0 1.2 copy-start.11
  108.0 1.2 copy-start.14
  125.0 1.1 copy-start.2
  126.2 1.5 copy-start.13
where the time goes:
time: 271 us; the launch traced here: 270 us
  blocking collectives  140 us (52%)
  waiting for transfers between devices  56.3 us (21%)
  starting transfers between devices  23.9 us (9%)
  other arithmetic  18.7 us (7%)
  matrix products  13.5 us (5%)
  local copies, waits for them, and re-layouts  12.7 us (5%)
  between operations  4.52 us (2%)
    psum x1, blocking collectives, per_device(): hidden_out = lax.psum(terms, 'tp').astype(jnp.bfloat16)  140 us
    ppermute x5, waiting for transfers between devices, swapped(): return lax.ppermute(block, axis, route)  56.3 us
    ppermute x5, starting transfers between devices, swapped(): return lax.ppermute(block, axis, route)  23.9 us
    unnamed x41, local copies, waits for them, and re-layouts  8.1 us
    select_n x5, other arithmetic, route_block(): current = jnp.where(taken_rows[:, None], arrived, current)  7.4 us
    dot_general x4, matrix products, advance(): jnp.einsum('nhk,nhkv->nhv', keyvec, state, precision=lax.Precision.HIGHEST)  6.69 us
    dot_general x4, matrix products, advance(): jnp.einsum('nhk,nhkv->nhv', query, state, precision=lax.Precision.HIGHEST)  6.54 us
  transfers between devices with their start and end apart: 5, of which 5 were waited for; matrix products, arithmetic and copies ran while one was open for 0% of the time, Pallas kernels for 0%

commit v1 on v0

v1 whole, which is shorter than its diff:
```python
import functools

import jax
import jax.numpy as jnp
from jax import lax
from jax.experimental import pallas as pl
from jax.experimental.pallas import tpu as pltpu
from jax.sharding import PartitionSpec as P

MESH = pl.DeviceIdType.MESH
F32 = jnp.float32
BF16 = jnp.bfloat16
GROUPS, MOVE, PIECES, TILE, LANES = 32, 3, 16, 16, 128
CONV_PIECE = (2, 7, 12)
VMEM = pltpu.VMEM
HEAD = 128


def piece_holder(piece, core):
    return 2 * piece + lax.rem(core + piece // 4, 2)


def migrate_kernel(
    state, conv, partner, slots, out,
    rows_out, conv_rows, conv_out, held, conv_held, turned, conv_turned, landed, conv_landed,
    send1, recv1, csend1, crecv1, send2, recv2, csend2, crecv2,
):
    me = lax.axis_index("req")
    core = lax.rem(lax.axis_index("tp"), 2)
    mine = me // 2
    holder = piece_holder(mine, core) == me

    barrier = pltpu.get_barrier_semaphore()

    def greet(k, carry):
        peer = lax.rem(me + k, GROUPS)
        pl.semaphore_signal(barrier, inc=1, device_id={"req": peer}, device_id_type=MESH)
        return carry

    lax.fori_loop(1, GROUPS, greet, 0)

    conv_rows[...] = jnp.zeros_like(conv_rows)
    for j in range(MOVE):
        slot = slots[0, j]
        for tap in range(3):
            for part in range(4):
                conv_rows[j, pl.ds(tap * 4 + part, 1), :] = conv[
                    slot, tap, :, part * LANES : (part + 1) * LANES
                ]
        conv_out[j] = conv_rows[j].astype(BF16)

    def pack(piece, carry):
        for j in range(MOVE):
            start = pl.multiple_of(lax.rem(piece, 8) * TILE, TILE)
            rows_out[piece, j] = state[slots[0, j], piece // 8, pl.ds(start, TILE), :].astype(BF16)
        return carry

    lax.fori_loop(0, PIECES, pack, 0)
    pl.semaphore_wait(barrier, GROUPS - 1)

    def first(piece, peer):
        return pltpu.make_async_remote_copy(
            src_ref=rows_out.at[piece], dst_ref=held.at[me], send_sem=send1.at[piece],
            recv_sem=recv1.at[me], device_id={"req": peer}, device_id_type=MESH,
        )

    def conv_first(j, peer):
        return pltpu.make_async_remote_copy(
            src_ref=conv_out.at[j], dst_ref=conv_held.at[me], send_sem=csend1.at[j],
            recv_sem=crecv1.at[me], device_id={"req": peer}, device_id_type=MESH,
        )

    def send_piece(k, carry):
        piece = lax.rem(mine + k, PIECES)
        peer = piece_holder(piece, core)

        @pl.when(peer != me)
        def _():
            first(piece, peer).start()

        @pl.when(peer == me)
        def _():
            held[me] = rows_out[piece]

        return carry

    lax.fori_loop(0, PIECES, send_piece, 0)
    for j in range(MOVE):
        peer = piece_holder(CONV_PIECE[j], core)

        @pl.when(peer != me)
        def _():
            conv_first(j, peer).start()

        @pl.when(peer == me)
        def _():
            conv_held[me] = conv_out[j]

    def second(dest):
        return pltpu.make_async_remote_copy(
            src_ref=turned.at[dest], dst_ref=landed.at[mine], send_sem=send2.at[dest],
            recv_sem=recv2.at[mine], device_id={"req": dest}, device_id_type=MESH,
        )

    def conv_second(j, dest):
        return pltpu.make_async_remote_copy(
            src_ref=conv_turned.at[dest], dst_ref=conv_landed.at[j], send_sem=csend2.at[dest],
            recv_sem=crecv2.at[j], device_id={"req": dest}, device_id_type=MESH,
        )

    def arrived(group):
        return pltpu.make_async_remote_copy(
            src_ref=rows_out.at[0], dst_ref=held.at[group], send_sem=send1.at[0],
            recv_sem=recv1.at[group], device_id={"req": group}, device_id_type=MESH,
        )

    def conv_arrived(group):
        return pltpu.make_async_remote_copy(
            src_ref=conv_out.at[0], dst_ref=conv_held.at[group], send_sem=csend1.at[0],
            recv_sem=crecv1.at[group], device_id={"req": group}, device_id_type=MESH,
        )

    @pl.when(holder)
    def _():
        def wait_first(k, carry):
            arrived(lax.rem(me + k, GROUPS)).wait_recv()
            return carry

        lax.fori_loop(1, GROUPS, wait_first, 0)

        def turn(k, carry):
            dest = lax.rem(me + k, GROUPS)
            for j in range(MOVE):
                turned[dest, j] = held[partner[j, dest], j]

            @pl.when(k > 0)
            def _():
                second(dest).start()

            return carry

        lax.fori_loop(0, GROUPS, turn, 0)
        landed[mine] = turned[me]

        for j in range(MOVE):

            @pl.when(mine == CONV_PIECE[j])
            def _():
                def wait_conv(k, carry):
                    conv_arrived(lax.rem(me + k, GROUPS)).wait_recv()
                    return carry

                lax.fori_loop(1, GROUPS, wait_conv, 0)

                def turn_conv(k, carry):
                    dest = lax.rem(me + k, GROUPS)
                    conv_turned[dest] = conv_held[partner[j, dest]]

                    @pl.when(k > 0)
                    def _():
                        conv_second(j, dest).start()

                    return carry

                lax.fori_loop(0, GROUPS, turn_conv, 0)
                conv_landed[j] = conv_turned[me]

    def wait_second(piece, carry):
        source = piece_holder(piece, core)

        @pl.when(source != me)
        def _():
            pltpu.make_async_remote_copy(
                src_ref=turned.at[0], dst_ref=landed.at[piece], send_sem=send2.at[0],
                recv_sem=recv2.at[piece], device_id={"req": source}, device_id_type=MESH,
            ).wait_recv()

        start = pl.multiple_of(piece * TILE, TILE)
        for j in range(MOVE):
            out[j, pl.ds(start, TILE), :] = landed[piece, j]
        return carry

    lax.fori_loop(0, PIECES, wait_second, 0)
    for j in range(MOVE):
        source = piece_holder(CONV_PIECE[j], core)

        @pl.when(source != me)
        def _():
            conv_second(j, source).wait_recv()

        out[j, PIECES * TILE :, :] = conv_landed[j]

    def done_first(piece, carry):
        peer = piece_holder(piece, core)

        @pl.when(peer != me)
        def _():
            first(piece, peer).wait_send()

        return carry

    lax.fori_loop(0, PIECES, done_first, 0)
    for j in range(MOVE):
        peer = piece_holder(CONV_PIECE[j], core)

        @pl.when(peer != me)
        def _():
            conv_first(j, peer).wait_send()

    @pl.when(holder)
    def _():
        def done_second(k, carry):
            second(lax.rem(me + k, GROUPS)).wait_send()
            return carry

        lax.fori_loop(1, GROUPS, done_second, 0)
        for j in range(MOVE):

            @pl.when(mine == CONV_PIECE[j])
            def _():
                def done_conv(k, carry):
                    conv_second(j, lax.rem(me + k, GROUPS)).wait_send()
                    return carry

                lax.fori_loop(1, GROUPS, done_conv, 0)


def migrate(state, conv, partner, slots):
    tile = (TILE, LANES)
    dma = pltpu.SemaphoreType.DMA
    return pl.pallas_call(
        migrate_kernel,
        out_shape=jax.ShapeDtypeStruct((MOVE, (PIECES + 1) * TILE, LANES), BF16),
        in_specs=[
            pl.BlockSpec(memory_space=VMEM),
            pl.BlockSpec(memory_space=VMEM),
            pl.BlockSpec(memory_space=pltpu.SMEM),
            pl.BlockSpec(memory_space=pltpu.SMEM),
        ],
        out_specs=pl.BlockSpec(memory_space=VMEM),
        scratch_shapes=[
            VMEM((PIECES, MOVE) + tile, BF16),
            VMEM((MOVE,) + tile, F32),
            VMEM((MOVE,) + tile, BF16),
            VMEM((GROUPS, MOVE) + tile, BF16),
            VMEM((GROUPS,) + tile, BF16),
            VMEM((GROUPS, MOVE) + tile, BF16),
            VMEM((GROUPS,) + tile, BF16),
            VMEM((PIECES, MOVE) + tile, BF16),
            VMEM((MOVE,) + tile, BF16),
            dma((PIECES,)), dma((GROUPS,)), dma((MOVE,)), dma((GROUPS,)),
            dma((GROUPS,)), dma((PIECES,)), dma((GROUPS,)), dma((MOVE,)),
        ],
        compiler_params=pltpu.CompilerParams(
            collective_id=0, has_side_effects=True, vmem_limit_bytes=32 << 20
        ),
        name="migrate",
    )(state, conv, partner, slots)


def halves(scalar_a, scalar_b, shape):
    lane = lax.broadcasted_iota(jnp.int32, shape, len(shape) - 1)
    return jnp.where(lane < HEAD, scalar_a, scalar_b)


def split16(value):
    high = value.astype(BF16)
    return high.astype(F32), value - high.astype(F32)


def advance_kernel(
    slots, decay_log, time_bias, state, came, conv, mixed, gates, zgate, weight, gain,
    new_state, new_conv, gated,
    taps, fresh, gate_rows, left, right, solved, flat, sems,
):
    rows = mixed.shape[0]
    copies = [
        pltpu.make_async_copy(state.at[pl.ds(2 * i, 2)], new_state.at[pl.ds(2 * i, 2)], sems.at[i])
        for i in range(rows // 2)
    ]
    for copy in copies:
        copy.start()

    for tap in range(3):
        taps[tap] = conv[:, tap]
    for j in range(MOVE):
        slot = slots[0, j]
        tile = came[j, PIECES * TILE :, :].astype(F32)
        for tap in range(3):
            for part in range(4):
                taps[tap, slot, :, part * LANES : (part + 1) * LANES] = tile[
                    tap * 4 + part : tap * 4 + part + 1, :
                ]
    fresh[...] = mixed[...].astype(F32)
    for tap in range(3):
        new_conv[:, tap, 0, :] = fresh[:, tap + 1, :]
    window = [taps[i, :, 0, :] for i in range(3)] + [fresh[:, t, :] for t in range(4)]

    gate_rows[...] = jnp.zeros_like(gate_rows)
    for t in range(4):
        for kind in range(2):
            at = t * 4 + kind * 2
            gate_rows[at : at + 2, 0:rows] = gates[t, kind]
    columns = gate_rows[...].T

    def column(at):
        return jnp.broadcast_to(columns[0:rows, at : at + 1], (rows, HEAD))

    def both(at):
        return jnp.concatenate([column(at), column(at + 1)], axis=1)

    rate = jnp.exp(halves(decay_log[0], decay_log[1], (1, 2 * HEAD)))
    bias = halves(time_bias[0], time_bias[1], (1, 2 * HEAD))
    keys, queries, values, decays, betas = [], [], [], [], []
    for t in range(4):
        total = window[t] * weight[0, 0:1, :]
        for tap in range(1, 4):
            total = total + window[t + tap] * weight[0, tap : tap + 1, :]
        c = total * jax.nn.sigmoid(total)
        q, k = c[:, :HEAD], c[:, HEAD : 2 * HEAD]
        queries.append(
            q * lax.rsqrt(jnp.sum(q * q, -1, keepdims=True) + 1e-06) / jnp.sqrt(jnp.float32(HEAD))
        )
        keys.append(k * lax.rsqrt(jnp.sum(k * k, -1, keepdims=True) + 1e-06))
        values.append(c[:, 2 * HEAD :])
        a = both(t * 4) + bias
        soft = jnp.maximum(a, 0.0) + jnp.log1p(jnp.exp(-jnp.abs(a)))
        decays.append(jnp.exp(-rate * soft))
        betas.append(jax.nn.sigmoid(both(t * 4 + 2)))

    left[...] = jnp.zeros_like(left)
    right[...] = jnp.zeros_like(right)
    key_parts = [split16(k) for k in keys]
    query_parts = [split16(q) for q in queries]
    for t in range(4):
        left[t, 0:rows, :] = key_parts[t][0]
        left[4 + t, 0:rows, :] = query_parts[t][0]
        left[8 + t, 0:rows, :] = key_parts[t][1]
        left[12 + t, 0:rows, :] = query_parts[t][1]

    for copy in copies:
        copy.wait()
    for j in range(MOVE):
        for h in range(2):
            new_state[slots[0, j], h] = came[j, h * HEAD : (h + 1) * HEAD, :].astype(F32)

    for r in range(rows):
        lhs = left[:, r, :].astype(BF16)
        for h in range(2):
            block = new_state[r, h]
            high = block.astype(BF16)
            low = (block - high.astype(F32)).astype(BF16)
            product = jnp.dot(lhs, high, preferred_element_type=F32) + jnp.dot(
                lhs, low, preferred_element_type=F32
            )
            solved[r, :, h * HEAD : (h + 1) * HEAD] = product[0:8] + product[8:16]

    writes = []
    carried = [decays[0]]
    for t in range(1, 4):
        carried.append(carried[-1] * decays[t])
    for t in range(4):
        read = solved[:, t, :] * carried[t]
        out = solved[:, 4 + t, :] * carried[t]
        writes = [w * decays[t] for w in writes]
        for s in range(t):
            read = read + writes[s] * jnp.sum(keys[t] * keys[s], -1, keepdims=True)
            out = out + writes[s] * jnp.sum(queries[t] * keys[s], -1, keepdims=True)
        writes.append((values[t] - read) * betas[t])
        out = out + writes[t] * jnp.sum(queries[t] * keys[t], -1, keepdims=True)
        square = out * out
        norm = jnp.concatenate(
            [
                jnp.broadcast_to(
                    lax.rsqrt(
                        jnp.mean(square[:, h * HEAD : (h + 1) * HEAD], -1, keepdims=True) + 1e-06
                    ),
                    (rows, HEAD),
                )
                for h in range(2)
            ],
            axis=1,
        )
        z = zgate[:, t, :].astype(F32)
        spread = jnp.concatenate([gain[...], gain[...]], axis=1)
        result = out * norm * spread * (z * jax.nn.sigmoid(z))
        for h in range(2):
            flat[h, pl.ds(t, rows, stride=4), :] = result[:, h * HEAD : (h + 1) * HEAD]
    for h in range(2):
        gated[:, h * HEAD : (h + 1) * HEAD] = flat[h].astype(BF16)

    left[12:16] = jnp.zeros_like(left[12:16])
    for t in range(4):
        left[4 + t, 0:rows, :] = key_parts[t][0]
        high, low = split16(writes[t])
        right[t, 0:rows, :] = high
        right[4 + t, 0:rows, :] = low
        right[8 + t, 0:rows, :] = high
    right[12, 0:rows, :] = carried[3]

    for r in range(rows):
        lhs = left[:, r, :].astype(BF16)
        rhs = right[:, r, :]
        update = lax.dot_general(
            lhs, rhs.astype(BF16), (((0,), (0,)), ((), ())), preferred_element_type=F32
        )
        for h in range(2):
            cut = slice(h * HEAD, (h + 1) * HEAD)
            new_state[r, h] = new_state[r, h] * rhs[12:13, cut] + update[:, cut]


def advance(slots, decay_log, time_bias, state, came, conv, mixed, gates, zgate, weight, gain):
    rows = state.shape[0]
    vmem = pl.BlockSpec(memory_space=VMEM)
    smem = pl.BlockSpec(memory_space=pltpu.SMEM)
    return pl.pallas_call(
        advance_kernel,
        out_shape=(
            jax.ShapeDtypeStruct(state.shape, F32),
            jax.ShapeDtypeStruct(conv.shape, F32),
            jax.ShapeDtypeStruct((rows * 4, 2 * HEAD), BF16),
        ),
        in_specs=[smem, smem, smem, pl.BlockSpec(memory_space=pl.ANY)] + [vmem] * 7,
        out_specs=(vmem, vmem, vmem),
        scratch_shapes=[
            VMEM((3, rows, 1, 4 * HEAD), F32),
            VMEM(mixed.shape, F32),
            VMEM((LANES, LANES), F32),
            VMEM((16, 16, HEAD), F32),
            VMEM((16, 16, 2 * HEAD), F32),
            VMEM((rows, 8, 2 * HEAD), F32),
            VMEM((2, rows * 4, HEAD), F32),
            pltpu.SemaphoreType.DMA((rows // 2,)),
        ],
        compiler_params=pltpu.CompilerParams(vmem_limit_bytes=32 << 20),
        name="advance",
    )(slots, decay_log, time_bias, state, came, conv, mixed, gates, zgate, weight, gain)


def reduce_kernel(
    gated, weight, out,
    give, own, got, pass_on, passed, half, half_got, blocks,
    give_send, give_recv, pass_send, pass_recv, half_send, half_recv,
    ring_send, ring_recv, mate_send, mate_recv,
):
    tp = lax.axis_index("tp")
    x, high, core = tp // 4, lax.rem(tp // 2, 2), lax.rem(tp, 2)
    mate = x * 4 + high * 2 + (1 - core)
    far = x * 4 + (1 - high) * 2 + core
    width = give.shape[2]

    def at_x(k):
        return lax.rem(x + k, 4)

    def ring(k):
        return at_x(k) * 4 + high * 2 + core

    barrier = pltpu.get_barrier_semaphore()
    for peer in (mate, far, ring(1), ring(2), ring(3)):
        pl.semaphore_signal(barrier, inc=1, device_id={"tp": peer}, device_id_type=MESH)

    def term(block):
        cut = pl.ds(pl.multiple_of(block * width, width), width)
        return jnp.dot(gated[...], weight[:, cut], preferred_element_type=F32)

    def to(peer, src, dst, send, recv):
        return pltpu.make_async_remote_copy(
            src_ref=src, dst_ref=dst, send_sem=send, recv_sem=recv,
            device_id={"tp": peer}, device_id_type=MESH,
        )

    order = (2, 1, 3, 0)
    gives = [to(mate, give.at[k], got.at[k], give_send.at[k], give_recv.at[k]) for k in range(4)]
    for k in order:
        give[k] = term(at_x(k) * 2 + 1 - core).astype(BF16)
        if k == order[0]:
            pl.semaphore_wait(barrier, 5)
        gives[k].start()
    for k in order:
        own[k] = term(at_x(k) * 2 + core)
    passes = [
        to(ring(k), pass_on.at[k - 1], passed.at[k - 1], pass_send.at[k - 1], pass_recv.at[k - 1])
        for k in range(1, 4)
    ]
    for k in order:
        gives[k].wait_recv()
        total = own[k] + got[k].astype(F32)
        if k:
            pass_on[k - 1] = total.astype(BF16)
            passes[k - 1].start()
    for k in range(1, 4):
        passes[k - 1].wait_recv()
        total = total + passed[k - 1].astype(F32)
    half[...] = total.astype(BF16)
    swap = to(far, half, half_got, half_send, half_recv)
    swap.start()
    swap.wait_recv()
    mine = x * 2 + core
    blocks[mine] = (half[...].astype(F32) + half_got[...].astype(F32)).astype(BF16)
    rings = [
        to(ring(k), blocks.at[mine], blocks.at[mine], ring_send.at[k - 1], ring_recv.at[k - 1])
        for k in range(1, 4)
    ]
    mates = [
        to(mate, blocks.at[at_x(k) * 2 + core], blocks.at[at_x(k) * 2 + core],
           mate_send.at[k], mate_recv.at[k])
        for k in range(4)
    ]
    for k in (2, 1, 3):
        rings[k - 1].start()
    mates[0].start()
    for k in range(1, 4):
        rings[k - 1].wait_recv()
        mates[4 - k].start()
    for k in range(4):
        mates[k].wait_recv()
    for block in range(8):
        out[:, block * width : (block + 1) * width] = blocks[block]
    for copy in gives + passes + [swap] + rings + mates:
        copy.wait_send()


def reduce_terms(gated, weight):
    rows, cols = gated.shape[0], weight.shape[1]
    block = (rows, cols // 8)
    vmem = pl.BlockSpec(memory_space=VMEM)
    dma = pltpu.SemaphoreType.DMA
    return pl.pallas_call(
        reduce_kernel,
        out_shape=jax.ShapeDtypeStruct((rows, cols), BF16),
        in_specs=[vmem, vmem],
        out_specs=vmem,
        scratch_shapes=[
            VMEM((4,) + block, BF16), VMEM((4,) + block, F32), VMEM((4,) + block, BF16),
            VMEM((3,) + block, BF16), VMEM((3,) + block, BF16),
            VMEM(block, BF16), VMEM(block, BF16), VMEM((8,) + block, BF16),
            dma((4,)), dma((4,)), dma((3,)), dma((3,)), dma, dma,
            dma((3,)), dma((3,)), dma((4,)), dma((4,)),
        ],
        compiler_params=pltpu.CompilerParams(
            collective_id=1, has_side_effects=True, vmem_limit_bytes=32 << 20
        ),
        name="reduce_terms",
    )(gated, weight)


def per_device(
    state,
    conv_state,
    mixed,
    gates,
    output_gate,
    conv_weight,
    decay_log,
    time_bias,
    norm_gain,
    out_weight,
    partner,
    moved_slots,
):
    conv = conv_state.transpose(0, 2, 1, 3)
    fresh = mixed.reshape(mixed.shape[0], mixed.shape[1], mixed.shape[3])
    gate_rows = gates.transpose(1, 2, 3, 0)
    came = migrate(state, conv, partner.T, moved_slots)
    new_state, new_conv, gated = advance(
        moved_slots, decay_log, time_bias, state, came, conv, fresh, gate_rows, output_gate,
        conv_weight, norm_gain.reshape(1, -1),
    )
    hidden = reduce_terms(gated, out_weight)
    hidden = hidden.reshape(mixed.shape[0], mixed.shape[1], -1)
    return (hidden, new_state, new_conv.transpose(0, 2, 1, 3))


def solution(mesh):
    placed = (
        P("req", "tp", None, None),
        P("req", "tp", None, None),
        P("req", None, "tp", None),
        P("req", None, None, "tp"),
        P("req", None, "tp"),
        P("tp", None, None),
        P("tp"),
        P("tp"),
        P(),
        P("tp", None),
        P(),
        P("req", None),
    )
    return jax.shard_map(
        per_device,
        mesh=mesh,
        in_specs=placed,
        out_specs=(P("req", None, None), P("req", "tp", None, None), P("req", "tp", None, None)),
        check_vma=False,
    )
```

time: 271 us -> 73.8 us (0.27)
  the two profiles are of different devices: /device:TPU:24 before, /device:TPU:1 now
where the time goes in v1:
time: 73.8 us; the launch traced here: 73.5 us
  Pallas kernels  68.3 us (93%)
  local copies, waits for them, and re-layouts  4.43 us (6%)
  between operations  0.79 us (1%)
    pallas_call x1, Pallas kernels, migrate(): pl.pallas_call(migrate_kernel, out_shape=jax.ShapeDtypeStruct((MOVE, (PIE...  39.4 us
    pallas_call x1, Pallas kernels, reduce_terms(): pl.pallas_call(reduce_kernel, out_shape=jax.ShapeDtypeStruct((rows, cols)...  25.6 us
    unnamed x26, local copies, waits for them, and re-layouts  3.67 us
    pallas_call x1, Pallas kernels, advance(): pl.pallas_call(advance_kernel, out_shape=(jax.ShapeDtypeStruct(state.shap...  3.24 us

profile of v1, /device:TPU:1, one launch (start us, length us, event | category | flops | bytes accessed | tf_op | source)
XLA Modules:
  0.0 73.5 jit_solution(3447930124336390165)
XLA Ops:
  0.6 0.0 copy-start.9
  0.6 0.0 copy-start.10
  0.7 0.0 copy-start.5
  0.7 0.0 copy-start
  0.7 1.4 %copy-done = f32[12,2,128,128]{3,2,1,0:T(8,128)S(1)} copy-done((f32[12,2,128,128]{3,2,1,0:T(8,128)S(1)}, f32[12,2,128,128]{3,2,1,0:T(8,128)}, u32[]{:S(2)}) %copy-start) | copy-done | bytes 1572888
  2.1 0.0 copy-start.2
  2.1 0.9 %copy-done.2 = f32[12,1,3,512]{3,1,2,0:T(1,128)S(1)} copy-done((f32[12,1,3,512]{3,1,2,0:T(1,128)S(1)}, f32[12,1,3,512]{3,1,2,0:T(1,128)}, u32[]{:S(2)}) %copy-start.2) | copy-done | bytes 73752
  3.0 0.0 copy-start.7
  3.0 0.7 copy-done.7
  3.7 0.0 copy-start.8
  3.7 0.7 copy-done.8
  4.3 0.0 copy-start.3
  4.3 0.0 copy-start.4
  4.3 0.0 copy-start.6
  4.3 0.0 copy-start.11
  4.3 0.0 copy-start.12
  4.3 0.0 copy-start.1
  4.3 39.4 %migrate.1.came = bf16[3,272,128]{2,1,0:T(8,128)(2,1)S(1)} custom-call(f32[12,2,128,128]{3,2,1,0:T(8,128)S(1)} %copy-done, f32[12,3,1,512]{3,2,1,0:T(1,128)S(1)} %bitcast.6, s32[3,32]{1,0:T(4,128)S(1)} %bitcast.10, s32[1,3]{1,0:T(1,128)S(1)} %copy-done.8), custom_call_target="tpu_custom_call" | custom-call | tf_op jit(solution)/shard_map/migrate/pallas_call | solution.py:231
  43.8 0.0 copy-done.9
  43.8 0.0 copy-done.10
  43.8 0.0 copy-done.5
  43.8 0.0 copy-done.3
  43.8 0.0 copy-done.4
  43.8 0.0 copy-done.6
  43.8 0.0 copy-done.11
  43.9 0.0 copy-done.12
  43.9 3.2 %advance.1 = (f32[12,2,128,128]{3,2,1,0:T(8,128)}, f32[12,3,1,512]{3,2,1,0:T(1,128)}, bf16[48,256]{1,0:T(8,128)(2,1)S(1)}) custom-call(s32[1,3]{1,0:T(1,128)S(1)} %copy-done.9, f32[2]{0:T(128)S(1)} %copy-done.10, f32[2]{0:T(128)S(1)} %copy-done.11, f32[12,2,128,128]{3,2,1,0:T(8,128)S(1)} %copy-done, bf16[3,272,128]{2,1,0:T(8,128)(2,1)S(1)} %migrate.1.came, ...), custom_call_target="tpu_custom_call" | custom-call | tf_op jit(solution)/shard_map/advance/pallas_call | solution.py:416
  47.1 0.0 copy-done.1
  47.1 25.6 %reduce_terms.1 = bf16[48,2048]{1,0:T(8,128)(2,1)S(1)} custom-call(bf16[48,256]{1,0:T(8,128)(2,1)S(1)} %get-tuple-element.6.gated, bf16[256,2048]{1,0:T(8,128)(2,1)S(1)} %copy-done.1), custom_call_target="tpu_custom_call" | custom-call | tf_op jit(solution)/shard_map/reduce_terms/pallas_call | solution.py:528
  72.8 0.8 %reshape.17 = bf16[12,4,2048]{2,1,0:T(4,128)(2,1)} reshape(bf16[48,2048]{1,0:T(8,128)(2,1)S(1)} %reduce_terms.1) | data formatting | bytes 393216 | tf_op jit(solution)/shard_map/reshape | solution.py:570
Async XLA Ops:
  0.6 43.1 %copy-start.9 = (s32[1,3]{1,0:T(1,128)S(1)}, s32[1,3]{1,0:T(1,128)}, u32[]{:S(2)}) copy-start(s32[1,3]{1,0:T(1,128)} %slots.3) | copy-start | bytes 40
  0.6 43.1 %copy-start.10 = (f32[2]{0:T(128)S(1)}, f32[2]{0:T(128)}, u32[]{:S(2)}) copy-start(f32[2]{0:T(128)} %decay_log.1) | copy-start | bytes 28
  0.7 43.1 %copy-start.5 = (f32[12,4,2,2]{0,3,2,1:T(2,128)S(1)}, f32[12,4,2,2]{0,3,2,1:T(2,128)}, u32[]{:S(2)}) copy-start(f32[12,4,2,2]{0,3,2,1:T(2,128)} %param.15) | copy-start | bytes 2308
  0.7 1.4 %copy-start = (f32[12,2,128,128]{3,2,1,0:T(8,128)S(1)}, f32[12,2,128,128]{3,2,1,0:T(8,128)}, u32[]{:S(2)}) copy-start(f32[12,2,128,128]{3,2,1,0:T(8,128)} %state.3) | copy-start | bytes 4718596
  2.1 0.9 %copy-start.2 = (f32[12,1,3,512]{3,1,2,0:T(1,128)S(1)}, f32[12,1,3,512]{3,1,2,0:T(1,128)}, u32[]{:S(2)}) copy-start(f32[12,1,3,512]{3,1,2,0:T(1,128)} %param.13) | copy-start | bytes 221188
  3.0 0.7 copy-start.7
  3.7 0.7 copy-start.8
  4.3 39.5 %copy-start.3 = (bf16[12,4,1,512]{3,1,2,0:T(4,128)(2,1)S(1)}, bf16[12,4,1,512]{3,1,2,0:T(4,128)(2,1)}, u32[]{:S(2)}) copy-start(bf16[12,4,1,512]{3,1,2,0:T(4,128)(2,1)} %param.14) | copy-start | bytes 147460
  4.3 39.5 %copy-start.4 = (bf16[12,4,256]{2,1,0:T(4,128)(2,1)S(1)}, bf16[12,4,256]{2,1,0:T(4,128)(2,1)}, u32[]{:S(2)}) copy-start(bf16[12,4,256]{2,1,0:T(4,128)(2,1)} %zgate.1) | copy-start | bytes 73732
  4.3 39.5 %copy-start.6 = (f32[1,4,512]{2,1,0:T(4,128)S(1)}, f32[1,4,512]{2,1,0:T(4,128)}, u32[]{:S(2)}) copy-start(f32[1,4,512]{2,1,0:T(4,128)} %weight.2) | copy-start | bytes 24580
  4.3 39.5 %copy-start.11 = (f32[2]{0:T(128)S(1)}, f32[2]{0:T(128)}, u32[]{:S(2)}) copy-start(f32[2]{0:T(128)} %time_bias.1) | copy-start | bytes 28
  4.3 39.5 %copy-start.12 = (f32[128]{0:T(128)S(1)}, f32[128]{0:T(128)}, u32[]{:S(2)}) copy-start(f32[128]{0:T(128)} %param.20) | copy-start | bytes 1540
  4.3 42.8 %copy-start.1 = (bf16[256,2048]{1,0:T(8,128)(2,1)S(1)}, bf16[256,2048]{1,0:T(8,128)(2,1)}, u32[]{:S(2)}) copy-start(bf16[256,2048]{1,0:T(8,128)(2,1)} %weight.3) | copy-start | bytes 3145732

commit v2 on v0

v2 whole, which is shorter than its diff:
```python
import jax
import jax.numpy as jnp
from jax import lax
from jax.experimental import pallas as pl
from jax.experimental.pallas import tpu as pltpu
from jax.sharding import PartitionSpec as P

MESH = pl.DeviceIdType.MESH
F32 = jnp.float32
BF16 = jnp.bfloat16
VMEM = pltpu.VMEM
GROUPS, MOVE, PIECES, TILE, LANES = 32, 3, 16, 16, 128
CONV_PIECE = (2, 7, 12)
HEAD, TAPS, STEPS = 128, 4, 4


def piece_holder(piece, core):
    return 2 * piece + lax.rem(core + piece // 4, 2)


def split16(value):
    high = value.astype(BF16)
    return high.astype(F32), value - high.astype(F32)


def halves(scalar_a, scalar_b, shape):
    lane = lax.broadcasted_iota(jnp.int32, shape, len(shape) - 1)
    return jnp.where(lane < HEAD, scalar_a, scalar_b)


def convolved(window, weight):
    queries, keys, values = [], [], []
    for t in range(STEPS):
        total = window[t] * weight[0, 0:1, :]
        for tap in range(1, TAPS):
            total = total + window[t + tap] * weight[0, tap : tap + 1, :]
        c = total * jax.nn.sigmoid(total)
        q, k = c[:, :HEAD], c[:, HEAD : 2 * HEAD]
        queries.append(
            q * lax.rsqrt(jnp.sum(q * q, -1, keepdims=True) + 1e-06) / jnp.sqrt(jnp.float32(HEAD))
        )
        keys.append(k * lax.rsqrt(jnp.sum(k * k, -1, keepdims=True) + 1e-06))
        values.append(c[:, 2 * HEAD :])
    return queries, keys, values


def read_side(left, queries, keys):
    rows = keys[0].shape[0]
    for t in range(STEPS):
        for at, part in enumerate(split16(keys[t]) + split16(queries[t])):
            left[t + (0, 8, 4, 12)[at], 0:rows, :] = part


def products(queries, keys):
    pairs = [(t, s) for t in range(STEPS) for s in range(t + 1)]
    written = {p: jnp.sum(keys[p[0]] * keys[p[1]], -1, keepdims=True) for p in pairs if p[0] != p[1]}
    read = {p: jnp.sum(queries[p[0]] * keys[p[1]], -1, keepdims=True) for p in pairs}
    return written, read


def solve(solved, flat, gram, values, decays, betas, zs, gain):
    rows = values[0].shape[0]
    key_key, query_key = gram
    writes = []
    carried = [decays[0]]
    for t in range(1, STEPS):
        carried.append(carried[-1] * decays[t])
    spread = jnp.concatenate([gain, gain], axis=1)
    for t in range(STEPS):
        read = solved[0:rows, t, :] * carried[t]
        out = solved[0:rows, 4 + t, :] * carried[t]
        writes = [w * decays[t] for w in writes]
        for s in range(t):
            read = read + writes[s] * key_key[t, s]
            out = out + writes[s] * query_key[t, s]
        writes.append((values[t] - read) * betas[t])
        out = out + writes[t] * query_key[t, t]
        square = out * out
        norm = jnp.concatenate(
            [
                jnp.broadcast_to(
                    lax.rsqrt(
                        jnp.mean(square[:, h * HEAD : (h + 1) * HEAD], -1, keepdims=True) + 1e-06
                    ),
                    (rows, HEAD),
                )
                for h in range(2)
            ],
            axis=1,
        )
        result = out * norm * spread * (zs[t] * jax.nn.sigmoid(zs[t]))
        for h in range(2):
            flat[h, pl.ds(t, rows, stride=STEPS), :] = result[:, h * HEAD : (h + 1) * HEAD]
    return writes, carried[-1]


def write_side(left, right, keys, writes, carried):
    rows = keys[0].shape[0]
    left[12:16] = jnp.zeros_like(left[12:16])
    for t in range(STEPS):
        high, low = split16(keys[t])
        left[t, 0:rows, :] = high
        left[4 + t, 0:rows, :] = high
        left[8 + t, 0:rows, :] = low
        high, low = split16(writes[t])
        right[t, 0:rows, :] = high
        right[4 + t, 0:rows, :] = low
        right[8 + t, 0:rows, :] = high
    right[12, 0:rows, :] = carried


def updated(left, right, row, blocks):
    lhs = left[:, row, :].astype(BF16)
    rhs = right[:, row, :]
    update = lax.dot_general(
        lhs, rhs.astype(BF16), (((0,), (0,)), ((), ())), preferred_element_type=F32
    )
    for h in range(2):
        cut = slice(h * HEAD, (h + 1) * HEAD)
        yield blocks[h] * rhs[12:13, cut] + update[:, cut]


class Reduction:
    def __init__(self, place, scratch, weight):
        self.x, self.high, self.core = place
        (
            self.give, self.own, self.got, self.pass_on, self.passed, self.half, self.half_got,
            self.blocks, gs, gr, ps, pr, hs, hr, rs, rr, ms, mr,
        ) = scratch
        self.weight = weight
        self.width = self.give.shape[2]
        mate, far = self.peers()[:2]
        self.gives = [self.to(mate, self.give.at[k], self.got.at[k], gs.at[k], gr.at[k]) for k in range(4)]
        self.passes = [
            self.to(self.ring(k), self.pass_on.at[k - 1], self.passed.at[k - 1], ps.at[k - 1], pr.at[k - 1])
            for k in range(1, 4)
        ]
        self.swap = self.to(far, self.half, self.half_got, hs, hr)
        self.mine = self.x * 2 + self.core
        own = self.blocks.at[self.mine]
        self.rings = [self.to(self.ring(k), own, own, rs.at[k - 1], rr.at[k - 1]) for k in range(1, 4)]
        self.mates = []
        for k in range(4):
            block = self.blocks.at[self.at_x(k) * 2 + self.core]
            self.mates.append(self.to(mate, block, block, ms.at[k], mr.at[k]))

    def peers(self):
        here = self.x * 4 + self.high * 2
        return (
            here + 1 - self.core, self.x * 4 + (1 - self.high) * 2 + self.core,
            self.ring(2), self.ring(1), self.ring(3),
        )

    def at_x(self, k):
        return lax.rem(self.x + k, 4)

    def ring(self, k):
        return self.at_x(k) * 4 + self.high * 2 + self.core

    def to(self, peer, src, dst, send, recv):
        return pltpu.make_async_remote_copy(
            src_ref=src, dst_ref=dst, send_sem=send, recv_sem=recv,
            device_id={"tp": peer}, device_id_type=MESH,
        )

    def term(self, gated, block):
        cut = pl.ds(pl.multiple_of(block * self.width, self.width), self.width)
        return jnp.dot(gated, self.weight[:, cut], preferred_element_type=F32)

    order = (2, 1, 3, 0)

    def begin(self, gated):
        for k in self.order:
            self.give[k] = self.term(gated, self.at_x(k) * 2 + 1 - self.core).astype(BF16)
            self.gives[k].start()
        for k in self.order:
            self.own[k] = self.term(gated, self.at_x(k) * 2 + self.core)

    def along_x(self):
        for k in self.order:
            self.gives[k].wait_recv()
            total = self.own[k] + self.got[k].astype(F32)
            if k:
                self.pass_on[k - 1] = total.astype(BF16)
                self.passes[k - 1].start()
            else:
                self.own[0] = total

    def along_z(self):
        total = self.own[0]
        for k in (1, 3, 2):
            self.passes[k - 1].wait_recv()
            total = total + self.passed[k - 1].astype(F32)
        self.half[...] = total.astype(BF16)
        self.swap.start()

    def back_x(self):
        self.swap.wait_recv()
        self.blocks[self.mine] = (self.half[...].astype(F32) + self.half_got[...].astype(F32)).astype(BF16)
        for k in (2, 1, 3):
            self.rings[k - 1].start()
        self.mates[0].start()

    def back_core(self):
        for k in (1, 3, 2):
            self.rings[k - 1].wait_recv()
            self.mates[4 - k].start()

    def end(self):
        for k in range(4):
            self.mates[k].wait_recv()

    def drain(self):
        for copy in self.gives + self.passes + [self.swap] + self.rings + self.mates:
            copy.wait_send()

    @staticmethod
    def scratch(rows, width):
        dma = pltpu.SemaphoreType.DMA
        block = (rows, width)
        return [
            VMEM((4,) + block, BF16), VMEM((4,) + block, F32), VMEM((4,) + block, BF16),
            VMEM((3,) + block, BF16), VMEM((3,) + block, BF16),
            VMEM(block, BF16), VMEM(block, BF16), VMEM((8,) + block, BF16),
            dma((4,)), dma((4,)), dma((3,)), dma((3,)), dma, dma,
            dma((3,)), dma((3,)), dma((4,)), dma((4,)),
        ]


class ShortReduction:
    def __init__(self, place, scratch, weight):
        self.x, self.high, self.core = place
        (
            self.give, self.own, self.got, self.half, self.half_got, self.blocks,
            gs, gr, hs, hr, bs, br,
        ) = scratch
        self.weight = weight
        self.width = self.give.shape[2]
        self.mine = self.x * 2 + self.core
        self.gives, self.backs, self.awaited = [], [], []
        for at, (dx, dc) in enumerate(self.order):
            peer = self.device(dx, dc)
            self.gives.append(self.to(peer, self.give.at[at], self.got.at[at], gs.at[at], gr.at[at]))
            own = self.blocks.at[self.mine]
            self.backs.append(self.to(peer, own, own, bs.at[at], br.at[at]))
            theirs = self.blocks.at[self.block(-dx, dc)]
            self.awaited.append(self.to(self.device(-dx, dc), own, theirs, bs.at[at], br.at[at]))
        far = self.x * 4 + (1 - self.high) * 2 + self.core
        self.swap = self.to(far, self.half, self.half_got, hs, hr)

    order = ((2, 0), (2, 1), (1, 0), (1, 1), (3, 0), (3, 1), (0, 1))

    def toward(self, dx, dc):
        return lax.rem(self.x + dx + 4, 4), 1 - self.core if dc else self.core

    def device(self, dx, dc):
        x, core = self.toward(dx, dc)
        return x * 4 + self.high * 2 + core

    def block(self, dx, dc):
        x, core = self.toward(dx, dc)
        return x * 2 + core

    def peers(self):
        far = self.x * 4 + (1 - self.high) * 2 + self.core
        return [far] + [self.device(dx, dc) for dx, dc in self.order]

    to = Reduction.to
    term = Reduction.term

    def begin(self, gated):
        for at, (dx, dc) in enumerate(self.order):
            self.give[at] = self.term(gated, self.block(dx, dc)).astype(BF16)
            self.gives[at].start()
        self.own[...] = self.term(gated, self.mine)

    def along_z(self):
        total = self.own[...]
        for at in (6, 2, 3, 4, 5, 0, 1):
            self.gives[at].wait_recv()
            total = total + self.got[at].astype(F32)
        self.half[...] = total.astype(BF16)
        self.swap.start()

    def back(self):
        self.swap.wait_recv()
        self.blocks[self.mine] = (self.half[...].astype(F32) + self.half_got[...].astype(F32)).astype(BF16)
        for copy in self.backs:
            copy.start()

    def end(self):
        for copy in self.awaited:
            copy.wait_recv()

    def drain(self):
        for copy in self.gives + [self.swap] + self.backs:
            copy.wait_send()

    @staticmethod
    def scratch(rows, width):
        dma = pltpu.SemaphoreType.DMA
        block = (rows, width)
        return [
            VMEM((7,) + block, BF16), VMEM(block, F32), VMEM((7,) + block, BF16),
            VMEM(block, BF16), VMEM(block, BF16), VMEM((8,) + block, BF16),
            dma((7,)), dma((7,)), dma, dma, dma((7,)), dma((7,)),
        ]


REDUCTION = 18


def decode_kernel(
    slots, partner, decay_log, time_bias,
    state_in, conv_in, mixed_in, gates_in, zgate_in, weight_in, gain_in, out_weight_in,
    states_out, hidden_all, hidden_moved,
    states, moved, store_sems, conv, mixed, gates, zgate, weight, gain, out_weight, load_sems,
    fresh, gate_rows, left, right, solved, flat, left_m, right_m, solved_m, flat_m,
    rows_out, conv_rows, conv_out, held_0, held_1, held_2, conv_held, turned, conv_turned, landed, conv_landed,
    send1, recv1, csend1, crecv1, send2, recv2, csend2, crecv2,
    *reductions,
):
    rows = mixed.shape[0]
    tp = lax.axis_index("tp")
    me = lax.axis_index("req")
    core = lax.rem(tp, 2)
    place = (tp // 4, lax.rem(tp // 2, 2), core)
    mine = me // 2
    holder = piece_holder(mine, core) == me
    held = (held_0, held_1, held_2)

    loads = [
        pltpu.make_async_copy(src, dst, load_sems.at[at])
        for at, (src, dst) in enumerate(
            (
                (conv_in, conv), (state_in, states), (mixed_in, mixed),
                (gates_in, gates), (weight_in, weight), (zgate_in, zgate), (gain_in, gain),
                (out_weight_in, out_weight),
            )
        )
    ]
    for load in loads:
        load.start()

    everyone = Reduction(place, reductions[:REDUCTION], out_weight)
    movers = ShortReduction(place, reductions[REDUCTION:], out_weight)
    barrier = pltpu.get_barrier_semaphore()

    def greet(k, carry):
        z, y = lax.rem(7 - lax.rem(me, 8) + k // 4, 8), lax.rem(me // 8 + 2 + k, 4)
        peer = y * 8 + z

        @pl.when(peer != me)
        def _():
            pl.semaphore_signal(barrier, inc=1, device_id={"req": peer}, device_id_type=MESH)

        return carry

    tp_peers = movers.peers()
    for peer in tp_peers:
        pl.semaphore_signal(barrier, inc=1, device_id={"tp": peer}, device_id_type=MESH)
    lax.fori_loop(0, GROUPS, greet, 0)

    loads[0].wait()
    conv_rows[...] = jnp.zeros_like(conv_rows)
    for j in range(MOVE):
        for tap in range(3):
            for part in range(4):
                conv_rows[j, pl.ds(tap * 4 + part, 1), :] = conv[
                    slots[0, j], tap, :, part * LANES : (part + 1) * LANES
                ]
        conv_out[j] = conv_rows[j].astype(BF16)
    loads[1].wait()

    def pack(piece, carry):
        start = pl.multiple_of(lax.rem(piece, 8) * TILE, TILE)
        for j in range(MOVE):
            rows_out[j, piece] = states[slots[0, j], piece // 8, pl.ds(start, TILE), :].astype(BF16)
        return carry

    lax.fori_loop(0, PIECES, pack, 0)

    for load in loads[2:7]:
        load.wait()
    fresh[...] = mixed[...].astype(F32)
    latest = [fresh[:, t, :] for t in range(STEPS)]
    gate_rows[...] = jnp.zeros_like(gate_rows)
    for t in range(STEPS):
        for kind in range(2):
            at = t * 4 + kind * 2
            gate_rows[at : at + 2, 0:rows] = gates[t, kind]
    columns = gate_rows[...].T

    def both(at):
        return jnp.concatenate(
            [
                jnp.broadcast_to(columns[0:rows, at + h : at + h + 1], (rows, HEAD))
                for h in range(2)
            ],
            axis=1,
        )

    rate = jnp.exp(halves(decay_log[0], decay_log[1], (1, 2 * HEAD)))
    bias = halves(time_bias[0], time_bias[1], (1, 2 * HEAD))
    decays, betas, zs = [], [], []
    for t in range(STEPS):
        a = both(t * 4) + bias
        soft = jnp.maximum(a, 0.0) + jnp.log1p(jnp.exp(-jnp.abs(a)))
        decays.append(jnp.exp(-rate * soft))
        betas.append(jax.nn.sigmoid(both(t * 4 + 2)))
        zs.append(zgate[:, t, :].astype(F32))
    spread = gain[...]

    left[...] = jnp.zeros_like(left)
    right[...] = jnp.zeros_like(right)
    window = [conv[:, tap, 0, :] for tap in range(3)] + latest
    queries, keys, values = convolved(window, weight)
    read_side(left, queries, keys)
    for r in range(rows):
        lhs = left[:, r, :].astype(BF16)
        for h in range(2):
            block = states[r, h]
            high = block.astype(BF16)
            low = (block - high.astype(F32)).astype(BF16)
            product = jnp.dot(lhs, high, preferred_element_type=F32) + jnp.dot(
                lhs, low, preferred_element_type=F32
            )
            solved[r, :, h * HEAD : (h + 1) * HEAD] = product[0:8] + product[8:16]
    gram = products(queries, keys)
    writes, carried = solve(solved, flat, gram, values, decays, betas, zs, spread)
    write_side(left, right, keys, writes, carried)

    def picked(value):
        at_row = lax.broadcasted_iota(jnp.int32, value.shape, 0)
        target = (8, value.shape[1])
        at_out = lax.broadcasted_iota(jnp.int32, target, 0)
        result = jnp.zeros(target, F32)
        for j in range(MOVE):
            row = jnp.sum(jnp.where(at_row == slots[0, j], value, 0.0), axis=0, keepdims=True)
            result = jnp.where(at_out == j, jnp.broadcast_to(row, target), result)
        return result

    latest_m = [picked(value) for value in latest]
    decays_m = [picked(value) for value in decays]
    betas_m = [picked(value) for value in betas]
    zs_m = [picked(value) for value in zs]

    pl.semaphore_wait(barrier, GROUPS - 1 + len(tp_peers))

    def first(j, piece, peer):
        return pltpu.make_async_remote_copy(
            src_ref=rows_out.at[j, piece], dst_ref=held[j].at[me], send_sem=send1.at[j, piece],
            recv_sem=recv1.at[j, me], device_id={"req": peer}, device_id_type=MESH,
        )

    def conv_first(j, peer):
        return pltpu.make_async_remote_copy(
            src_ref=conv_out.at[j], dst_ref=conv_held.at[me], send_sem=csend1.at[j],
            recv_sem=crecv1.at[me], device_id={"req": peer}, device_id_type=MESH,
        )

    for j in range(MOVE):
        peer = piece_holder(CONV_PIECE[j], core)

        @pl.when(peer != me)
        def _():
            conv_first(j, peer).start()

        @pl.when(peer == me)
        def _():
            conv_held[me] = conv_out[j]

    for j in range(MOVE):

        def send_piece(k, carry):
            piece = lax.rem(mine + k, PIECES)
            peer = piece_holder(piece, core)

            @pl.when(peer != me)
            def _():
                first(j, piece, peer).start()

            @pl.when(peer == me)
            def _():
                held[j][me] = rows_out[j, piece]

            return carry

        lax.fori_loop(0, PIECES, send_piece, 0)

    loads[7].wait()
    everyone.begin(jnp.concatenate([flat[0], flat[1]], axis=1).astype(BF16))
    for r in range(rows):
        new = list(updated(left, right, r, [states[r, h] for h in range(2)]))
        for h in range(2):
            states[r, h] = new[h]
    stores = [
        pltpu.make_async_copy(src, dst, store_sems.at[at])
        for at, (src, dst) in enumerate(
            (
                (states, states_out.at[pl.ds(0, rows)]), (everyone.blocks, hidden_all),
                (moved, states_out.at[pl.ds(rows, MOVE)]),
                (movers.blocks, hidden_moved),
            )
        )
    ]
    stores[0].start()
    everyone.along_x()

    def second(j, dest):
        return pltpu.make_async_remote_copy(
            src_ref=turned.at[j, dest], dst_ref=landed.at[j, mine], send_sem=send2.at[j, dest],
            recv_sem=recv2.at[j, mine], device_id={"req": dest}, device_id_type=MESH,
        )

    def conv_second(j, dest):
        return pltpu.make_async_remote_copy(
            src_ref=conv_turned.at[dest], dst_ref=conv_landed.at[j], send_sem=csend2.at[dest],
            recv_sem=crecv2.at[j], device_id={"req": dest}, device_id_type=MESH,
        )

    for j in range(MOVE):

        @pl.when(holder)
        def _():
            def wait_first(k, carry):
                group = lax.rem(me + k, GROUPS)
                pltpu.make_async_remote_copy(
                    src_ref=rows_out.at[j, 0], dst_ref=held[j].at[group], send_sem=send1.at[j, 0],
                    recv_sem=recv1.at[j, group], device_id={"req": group}, device_id_type=MESH,
                ).wait_recv()
                return carry

            lax.fori_loop(1, GROUPS, wait_first, 0)

            def turn(k, carry):
                dest = lax.rem(me + k, GROUPS)
                turned[j, dest] = held[j][partner[j, dest]]

                @pl.when(k > 0)
                def _():
                    second(j, dest).start()

                return carry

            lax.fori_loop(0, GROUPS, turn, 0)
            landed[j, mine] = turned[j, me]

        @pl.when(jnp.logical_and(holder, mine == CONV_PIECE[j]))
        def _():
            def wait_conv(k, carry):
                group = lax.rem(me + k, GROUPS)
                pltpu.make_async_remote_copy(
                    src_ref=conv_out.at[0], dst_ref=conv_held.at[group], send_sem=csend1.at[0],
                    recv_sem=crecv1.at[group], device_id={"req": group}, device_id_type=MESH,
                ).wait_recv()
                return carry

            lax.fori_loop(1, GROUPS, wait_conv, 0)

            def turn_conv(k, carry):
                dest = lax.rem(me + k, GROUPS)
                conv_turned[dest] = conv_held[partner[j, dest]]

                @pl.when(k > 0)
                def _():
                    conv_second(j, dest).start()

                return carry

            lax.fori_loop(0, GROUPS, turn_conv, 0)
            conv_landed[j] = conv_turned[me]

    everyone.along_z()

    for j in range(MOVE):
        source = piece_holder(CONV_PIECE[j], core)

        @pl.when(source != me)
        def _():
            conv_second(j, source).wait_recv()

    at_out = lax.broadcasted_iota(jnp.int32, (8, LANES), 0)
    window_m = []
    for tap in range(3):
        parts = []
        for part in range(4):
            at = tap * 4 + part
            value = jnp.zeros((8, LANES), F32)
            for j in range(MOVE):
                row = conv_landed[j].astype(F32)[at : at + 1, :]
                value = jnp.where(at_out == j, jnp.broadcast_to(row, (8, LANES)), value)
            parts.append(value)
        window_m.append(jnp.concatenate(parts, axis=1))
    left_m[...] = jnp.zeros_like(left_m)
    right_m[...] = jnp.zeros_like(right_m)
    solved_m[...] = jnp.zeros_like(solved_m)
    queries, keys, values = convolved(window_m + latest_m, weight)
    read_side(left_m, queries, keys)
    gram = products(queries, keys)

    for j in range(MOVE):

        def wait_second(piece, carry):
            source = piece_holder(piece, core)

            @pl.when(source != me)
            def _():
                pltpu.make_async_remote_copy(
                    src_ref=turned.at[j, 0], dst_ref=landed.at[j, piece], send_sem=send2.at[j, 0],
                    recv_sem=recv2.at[j, piece], device_id={"req": source}, device_id_type=MESH,
                ).wait_recv()

            return carry

        lax.fori_loop(0, PIECES, wait_second, 0)
        lhs = left_m[:, j, :].astype(BF16)
        for h in range(2):
            block = landed[j, h * 8 : (h + 1) * 8].reshape(HEAD, HEAD)
            product = jnp.dot(lhs, block, preferred_element_type=F32)
            solved_m[j, :, h * HEAD : (h + 1) * HEAD] = product[0:8] + product[8:16]

    writes, carried = solve(
        solved_m, flat_m, gram, values, decays_m, betas_m, zs_m, spread
    )
    movers.begin(jnp.concatenate([flat_m[0, 0:16], flat_m[1, 0:16]], axis=1).astype(BF16))
    write_side(left_m, right_m, keys, writes, carried)
    movers.along_z()
    everyone.back_x()
    for j in range(MOVE):
        blocks = [
            landed[j, h * 8 : (h + 1) * 8].reshape(HEAD, HEAD).astype(F32) for h in range(2)
        ]
        for h, new in enumerate(updated(left_m, right_m, j, blocks)):
            moved[j, h] = new
    stores[2].start()
    everyone.back_core()

    def done_first(piece, carry):
        peer = piece_holder(piece, core)

        @pl.when(peer != me)
        def _():
            for j in range(MOVE):
                first(j, piece, peer).wait_send()

        return carry

    lax.fori_loop(0, PIECES, done_first, 0)
    for j in range(MOVE):
        peer = piece_holder(CONV_PIECE[j], core)

        @pl.when(peer != me)
        def _():
            conv_first(j, peer).wait_send()

    @pl.when(holder)
    def _():
        def done_second(k, carry):
            for j in range(MOVE):
                second(j, lax.rem(me + k, GROUPS)).wait_send()
            return carry

        lax.fori_loop(1, GROUPS, done_second, 0)
        for j in range(MOVE):

            @pl.when(mine == CONV_PIECE[j])
            def _():
                def done_conv(k, carry):
                    conv_second(j, lax.rem(me + k, GROUPS)).wait_send()
                    return carry

                lax.fori_loop(1, GROUPS, done_conv, 0)

    everyone.end()
    stores[1].start()
    everyone.drain()
    movers.back()
    movers.end()
    stores[3].start()
    movers.drain()
    for store in stores:
        store.wait()


def decode(
    slots, partner, decay_log, time_bias, state, conv, mixed, gates, zgate, weight, gain, out_weight
):
    rows = state.shape[0]
    width = out_weight.shape[1] // 8
    tile = (TILE, LANES)
    dma = pltpu.SemaphoreType.DMA
    smem = pl.BlockSpec(memory_space=pltpu.SMEM)
    anywhere = pl.BlockSpec(memory_space=pl.ANY)
    arrays = (state, conv, mixed, gates, zgate, weight, gain, out_weight)

    def working(count, padded):
        return [
            VMEM((16, padded, HEAD), F32),
            VMEM((16, padded, 2 * HEAD), F32),
            VMEM((count, 8, 2 * HEAD), F32),
            VMEM((2, count * STEPS, HEAD), F32),
        ]

    return pl.pallas_call(
        decode_kernel,
        out_shape=(
            jax.ShapeDtypeStruct((rows + MOVE,) + state.shape[1:], F32),
            jax.ShapeDtypeStruct((8, rows * STEPS, width), BF16),
            jax.ShapeDtypeStruct((8, TILE, width), BF16),
        ),
        in_specs=[smem] * 4 + [anywhere] * len(arrays),
        out_specs=(anywhere,) * 3,
        scratch_shapes=[VMEM(state.shape, F32), VMEM((MOVE,) + state.shape[1:], F32), dma((4,))]
        + [VMEM(a.shape, a.dtype) for a in arrays[1:]]
        + [dma((len(arrays),)), VMEM(mixed.shape, F32), VMEM((LANES, LANES), F32)]
        + working(rows, 16)
        + working(8, 8)
        + [
            VMEM((MOVE, PIECES) + tile, BF16),
            VMEM((MOVE,) + tile, F32),
            VMEM((MOVE,) + tile, BF16),
            VMEM((GROUPS,) + tile, BF16),
            VMEM((GROUPS,) + tile, BF16),
            VMEM((GROUPS,) + tile, BF16),
            VMEM((GROUPS,) + tile, BF16),
            VMEM((MOVE, GROUPS) + tile, BF16),
            VMEM((GROUPS,) + tile, BF16),
            VMEM((MOVE, PIECES) + tile, BF16),
            VMEM((MOVE,) + tile, BF16),
            dma((MOVE, PIECES)), dma((MOVE, GROUPS)), dma((MOVE,)), dma((GROUPS,)),
            dma((MOVE, GROUPS)), dma((MOVE, PIECES)), dma((GROUPS,)), dma((MOVE,)),
        ]
        + Reduction.scratch(rows * STEPS, width)
        + ShortReduction.scratch(TILE, width),
        compiler_params=pltpu.CompilerParams(
            collective_id=0, has_side_effects=True, vmem_limit_bytes=58 << 20
        ),
        name="decode",
    )(slots, partner, decay_log, time_bias, *arrays)


def place_kernel(
    slots, states, hidden_all, hidden_moved, mixed, hidden, new_state, new_conv,
    held, kept, changed, latest, fresh, out, load_sems, store_sems,
):
    rows = mixed.shape[0]
    width = hidden_all.shape[2]
    loads, stores = [], []
    for r in range(rows):
        source = r
        for j in range(MOVE):
            source = jnp.where(slots[0, j] == r, rows + j, source)
        loads.append(pltpu.make_async_copy(states.at[source], held.at[r], load_sems.at[r]))
        stores.append(pltpu.make_async_copy(held.at[r], new_state.at[r], store_sems.at[r]))
    for at, (src, dst) in enumerate(((hidden_all, kept), (hidden_moved, changed), (mixed, latest))):
        loads.append(pltpu.make_async_copy(src, dst, load_sems.at[rows + at]))
    stores.append(pltpu.make_async_copy(out, hidden, store_sems.at[rows]))
    stores.append(pltpu.make_async_copy(fresh, new_conv, store_sems.at[rows + 1]))
    for load in loads[rows:] + loads[:rows]:
        load.start()
    for r in range(rows):
        loads[r].wait()
        stores[r].start()
    for load in loads[rows:]:
        load.wait()
    values = latest[...].astype(F32)
    for tap in range(3):
        fresh[:, tap, 0, :] = values[:, tap + 1, :]
    stores[rows + 1].start()
    for block in range(8):
        cut = slice(block * width, (block + 1) * width)
        stay = kept[block].astype(F32)
        came = changed[block].astype(F32)
        for r in range(rows):
            value = stay[r * STEPS : (r + 1) * STEPS, :]
            for j in range(MOVE):
                value = jnp.where(slots[0, j] == r, came[j * STEPS : (j + 1) * STEPS, :], value)
            out[r, :, cut] = value.astype(BF16)
    stores[rows].start()
    for store in stores:
        store.wait()


def place(slots, states, hidden_all, hidden_moved, mixed):
    rows = mixed.shape[0]
    dma = pltpu.SemaphoreType.DMA
    anywhere = pl.BlockSpec(memory_space=pl.ANY)
    hidden = (rows, STEPS, 8 * hidden_all.shape[2])
    conv = (rows, TAPS - 1, 1, mixed.shape[2])
    return pl.pallas_call(
        place_kernel,
        out_shape=(
            jax.ShapeDtypeStruct(hidden, BF16),
            jax.ShapeDtypeStruct((rows,) + states.shape[1:], F32),
            jax.ShapeDtypeStruct(conv, F32),
        ),
        in_specs=[pl.BlockSpec(memory_space=pltpu.SMEM)] + [anywhere] * 4,
        out_specs=(anywhere,) * 3,
        scratch_shapes=[
            VMEM((rows,) + states.shape[1:], F32), VMEM(hidden_all.shape, BF16),
            VMEM(hidden_moved.shape, BF16), VMEM(mixed.shape, BF16), VMEM(conv, F32),
            VMEM(hidden, BF16), dma((rows + 3,)), dma((rows + 2,)),
        ],
        compiler_params=pltpu.CompilerParams(vmem_limit_bytes=58 << 20),
        name="place",
    )(slots, states, hidden_all, hidden_moved, mixed)


def per_device(
    state,
    conv_state,
    mixed,
    gates,
    output_gate,
    conv_weight,
    decay_log,
    time_bias,
    norm_gain,
    out_weight,
    partner,
    moved_slots,
):
    fresh = mixed.reshape(mixed.shape[0], mixed.shape[1], mixed.shape[3])
    states, hidden_all, hidden_moved = decode(
        moved_slots, partner.T, decay_log, time_bias, state, conv_state.transpose(0, 2, 1, 3),
        fresh, gates.transpose(1, 2, 3, 0), output_gate, conv_weight, norm_gain.reshape(1, -1),
        out_weight,
    )
    hidden, new_state, new_conv = place(moved_slots, states, hidden_all, hidden_moved, fresh)
    return (hidden, new_state, new_conv.transpose(0, 2, 1, 3))


def solution(mesh):
    placed = (
        P("req", "tp", None, None),
        P("req", "tp", None, None),
        P("req", None, "tp", None),
        P("req", None, None, "tp"),
        P("req", None, "tp"),
        P("tp", None, None),
        P("tp"),
        P("tp"),
        P(),
        P("tp", None),
        P(),
        P("req", None),
    )
    return jax.shard_map(
        per_device,
        mesh=mesh,
        in_specs=placed,
        out_specs=(P("req", None, None), P("req", "tp", None, None), P("req", "tp", None, None)),
        check_vma=False,
    )
```

time: 271 us -> 66.2 us (0.24)
  the two profiles are of different devices: /device:TPU:24 before, /device:TPU:1 now
where the time goes in v2:
time: 66.2 us; the launch traced here: 65.9 us
  Pallas kernels  65.3 us (99%)
    pallas_call x1, Pallas kernels, decode(): pl.pallas_call(decode_kernel, out_shape=(jax.ShapeDtypeStruct((rows + MOV...  61.9 us
    pallas_call x1, Pallas kernels, place(): pl.pallas_call(place_kernel, out_shape=(jax.ShapeDtypeStruct(hidden, BF16...  3.41 us

profile of v2, /device:TPU:1, one launch (start us, length us, event | category | flops | bytes accessed | tf_op | source)
XLA Modules:
  0.0 65.9 jit_solution(12697441821180177785)
XLA Ops:
  0.6 61.9 %decode.1 = (f32[15,2,128,128]{3,2,1,0:T(8,128)}, bf16[8,48,256]{2,1,0:T(8,128)(2,1)}, bf16[8,16,256]{2,1,0:T(8,128)(2,1)}) custom-call(s32[1,3]{1,0:T(1,128)} %slots.3, s32[3,32]{1,0:T(4,128)} %bitcast.10, f32[2]{0:T(128)} %decay_log.1, f32[2]{0:T(128)} %time_bias.1, f32[12,2,128,128]{3,2,1,0:T(8,128)} %state_in.1, f32[12,3,1,512]{3,2,1,0:T(1,128)} %bitcast.8, ...), custom_call_target="tpu_custom_call" | custom-call | tf_op jit(solution)/shard_map/decode/pallas_call | solution.py:705
  62.5 3.4 %place.1 = (bf16[12,4,2048]{2,1,0:T(4,128)(2,1)}, f32[12,2,128,128]{3,2,1,0:T(8,128)}, f32[12,3,1,512]{3,2,1,0:T(1,128)}) custom-call(s32[1,3]{1,0:T(1,128)} %slots.3, f32[15,2,128,128]{3,2,1,0:T(8,128)} %get-tuple-element.9.states, bf16[8,48,256]{2,1,0:T(8,128)(2,1)} %get-tuple-element.10.hidden_all, bf16[8,16,256]{2,1,0:T(8,128)(2,1)} %get-tuple-element.11.hidden_moved, ...), custom_call_target="tpu_custom_call" | custom-call | tf_op jit(solution)/shard_map/place/pallas_call | solution.py:791

commit v3 on v2

--- a/solution.py
+++ b/solution.py
@@ -9,13 +9,30 @@
 F32 = jnp.float32
 BF16 = jnp.bfloat16
 VMEM = pltpu.VMEM
-GROUPS, MOVE, PIECES, TILE, LANES = 32, 3, 16, 16, 128
-CONV_PIECE = (2, 7, 12)
+GROUPS, MOVE, PIECES, TILE, LANES = 32, 3, 8, 16, 128
+PIECE = 2 * TILE
+CONV_PIECE = (1, 4, 7)
 HEAD, TAPS, STEPS = 128, 4, 4
 
 
-def piece_holder(piece, core):
-    return 2 * piece + lax.rem(core + piece // 4, 2)
+def piece_holder(piece):
+    return piece // 2 * 8 + 2 + 3 * lax.rem(piece, 2)
+
+
+def piece_at(group):
+    return group // 8 * 2 + lax.rem(group, 8) // 4
+
+
+def flipped(number, flips, bits):
+    result = 0
+    for bit in range(bits):
+        a, b = lax.rem(number // (1 << bit), 2), lax.rem(flips // (1 << bit), 2)
+        result = result + (a + b - 2 * a * b) * (1 << bit)
+    return result
+
+
+def crossing_first(me, k):
+    return lax.rem(me // 8 + k, 4) * 8 + flipped(lax.rem(me, 8), 7 - k // 4, 3)
 
 
 def split16(value):
@@ -325,8 +342,8 @@
     me = lax.axis_index("req")
     core = lax.rem(tp, 2)
     place = (tp // 4, lax.rem(tp // 2, 2), core)
-    mine = me // 2
-    holder = piece_holder(mine, core) == me
+    mine = piece_at(me)
+    holder = piece_holder(mine) == me
     held = (held_0, held_1, held_2)
 
     loads = [
@@ -347,10 +364,10 @@
     barrier = pltpu.get_barrier_semaphore()
 
     def greet(k, carry):
-        z, y = lax.rem(7 - lax.rem(me, 8) + k // 4, 8), lax.rem(me // 8 + 2 + k, 4)
-        peer = y * 8 + z
-
-        @pl.when(peer != me)
+        peer = crossing_first(me, k)
+        turns = piece_holder(piece_at(peer)) == peer
+
+        @pl.when(jnp.logical_and(peer != me, jnp.logical_or(holder, turns)))
         def _():
             pl.semaphore_signal(barrier, inc=1, device_id={"req": peer}, device_id_type=MESH)
 
@@ -373,12 +390,55 @@
     loads[1].wait()
 
     def pack(piece, carry):
-        start = pl.multiple_of(lax.rem(piece, 8) * TILE, TILE)
+        start = pl.multiple_of(lax.rem(piece, 4) * PIECE, PIECE)
         for j in range(MOVE):
-            rows_out[j, piece] = states[slots[0, j], piece // 8, pl.ds(start, TILE), :].astype(BF16)
+            rows_out[j, piece] = states[slots[0, j], piece // 4, pl.ds(start, PIECE), :].astype(BF16)
         return carry
 
     lax.fori_loop(0, PIECES, pack, 0)
+
+    pl.semaphore_wait(barrier, jnp.where(holder, GROUPS - 1, PIECES) + len(tp_peers))
+
+    def first(j, piece, peer):
+        return pltpu.make_async_remote_copy(
+            src_ref=rows_out.at[j, piece], dst_ref=held[j].at[me], send_sem=send1.at[j, piece],
+            recv_sem=recv1.at[j, me], device_id={"req": peer}, device_id_type=MESH,
+        )
+
+    def conv_first(j, peer):
+        return pltpu.make_async_remote_copy(
+            src_ref=conv_out.at[j], dst_ref=conv_held.at[me], send_sem=csend1.at[j],
+            recv_sem=crecv1.at[me], device_id={"req": peer}, device_id_type=MESH,
+        )
+
+    for j in range(MOVE):
+        peer = piece_holder(CONV_PIECE[j])
+
+        @pl.when(peer != me)
+        def _():
+            conv_first(j, peer).start()
+
+        @pl.when(peer == me)
+        def _():
+            conv_held[me] = conv_out[j]
+
+    for j in range(MOVE):
+
+        def send_piece(k, carry):
+            piece = lax.rem(mine // 2 + k, 4) * 2 + flipped(lax.rem(mine, 2), 1 - k // 4, 1)
+            peer = piece_holder(piece)
+
+            @pl.when(peer != me)
+            def _():
+                first(j, piece, peer).start()
+
+            @pl.when(peer == me)
+            def _():
+                held[j][me] = rows_out[j, piece]
+
+            return carry
+
+        lax.fori_loop(0, PIECES, send_piece, 0)
 
     for load in loads[2:7]:
         load.wait()
@@ -445,49 +505,6 @@
     betas_m = [picked(value) for value in betas]
     zs_m = [picked(value) for value in zs]
 
-    pl.semaphore_wait(barrier, GROUPS - 1 + len(tp_peers))
-
-    def first(j, piece, peer):
-        return pltpu.make_async_remote_copy(
-            src_ref=rows_out.at[j, piece], dst_ref=held[j].at[me], send_sem=send1.at[j, piece],
-            recv_sem=recv1.at[j, me], device_id={"req": peer}, device_id_type=MESH,
-        )
-
-    def conv_first(j, peer):
-        return pltpu.make_async_remote_copy(
-            src_ref=conv_out.at[j], dst_ref=conv_held.at[me], send_sem=csend1.at[j],
-            recv_sem=crecv1.at[me], device_id={"req": peer}, device_id_type=MESH,
-        )
-
-    for j in range(MOVE):
-        peer = piece_holder(CONV_PIECE[j], core)
-
-        @pl.when(peer != me)
-        def _():
-            conv_first(j, peer).start()
-
-        @pl.when(peer == me)
-        def _():
-            conv_held[me] = conv_out[j]
-
-    for j in range(MOVE):
-
-        def send_piece(k, carry):
-            piece = lax.rem(mine + k, PIECES)
-            peer = piece_holder(piece, core)
-
-            @pl.when(peer != me)
-            def _():
-                first(j, piece, peer).start()
-
-            @pl.when(peer == me)
-            def _():
-                held[j][me] = rows_out[j, piece]
-
-            return carry
-
-        lax.fori_loop(0, PIECES, send_piece, 0)
-
     loads[7].wait()
     everyone.begin(jnp.concatenate([flat[0], flat[1]], axis=1).astype(BF16))
     for r in range(rows):
@@ -505,7 +522,6 @@
         )
     ]
     stores[0].start()
-    everyone.along_x()
 
     def second(j, dest):
         return pltpu.make_async_remote_copy(
@@ -534,10 +550,10 @@
             lax.fori_loop(1, GROUPS, wait_first, 0)
 
             def turn(k, carry):
-                dest = lax.rem(me + k, GROUPS)
+                dest = crossing_first(me, k)
                 turned[j, dest] = held[j][partner[j, dest]]
 
-                @pl.when(k > 0)
+                @pl.when(dest != me)
                 def _():
                     second(j, dest).start()
 
@@ -559,10 +575,10 @@
             lax.fori_loop(1, GROUPS, wait_conv, 0)
 
             def turn_conv(k, carry):
-                dest = lax.rem(me + k, GROUPS)
+                dest = crossing_first(me, k)
                 conv_turned[dest] = conv_held[partner[j, dest]]
 
-                @pl.when(k > 0)
+                @pl.when(dest != me)
                 def _():
                     conv_second(j, dest).start()
 
@@ -571,10 +587,13 @@
             lax.fori_loop(0, GROUPS, turn_conv, 0)
             conv_landed[j] = conv_turned[me]
 
+        if j == 0:
+            everyone.along_x()
+
     everyone.along_z()
 
     for j in range(MOVE):
-        source = piece_holder(CONV_PIECE[j], core)
+        source = piece_holder(CONV_PIECE[j])
 
         @pl.when(source != me)
         def _():
@@ -602,7 +621,7 @@
     for j in range(MOVE):
 
         def wait_second(piece, carry):
-            source = piece_holder(piece, core)
+            source = piece_holder(piece)
 
             @pl.when(source != me)
             def _():
@@ -616,7 +635,7 @@
         lax.fori_loop(0, PIECES, wait_second, 0)
         lhs = left_m[:, j, :].astype(BF16)
         for h in range(2):
-            block = landed[j, h * 8 : (h + 1) * 8].reshape(HEAD, HEAD)
+            block = landed[j, h * 4 : (h + 1) * 4].reshape(HEAD, HEAD)
             product = jnp.dot(lhs, block, preferred_element_type=F32)
             solved_m[j, :, h * HEAD : (h + 1) * HEAD] = product[0:8] + product[8:16]
 
@@ -629,7 +648,7 @@
     everyone.back_x()
     for j in range(MOVE):
         blocks = [
-            landed[j, h * 8 : (h + 1) * 8].reshape(HEAD, HEAD).astype(F32) for h in range(2)
+            landed[j, h * 4 : (h + 1) * 4].reshape(HEAD, HEAD).astype(F32) for h in range(2)
         ]
         for h, new in enumerate(updated(left_m, right_m, j, blocks)):
             moved[j, h] = new
@@ -637,7 +656,7 @@
     everyone.back_core()
 
     def done_first(piece, carry):
-        peer = piece_holder(piece, core)
+        peer = piece_holder(piece)
 
         @pl.when(peer != me)
         def _():
@@ -648,7 +667,7 @@
 
     lax.fori_loop(0, PIECES, done_first, 0)
     for j in range(MOVE):
-        peer = piece_holder(CONV_PIECE[j], core)
+        peer = piece_holder(CONV_PIECE[j])
 
         @pl.when(peer != me)
         def _():
@@ -688,7 +707,7 @@
 ):
     rows = state.shape[0]
     width = out_weight.shape[1] // 8
-    tile = (TILE, LANES)
+    tile, rows_of = (TILE, LANES), (PIECE, LANES)
     dma = pltpu.SemaphoreType.DMA
     smem = pl.BlockSpec(memory_space=pltpu.SMEM)
     anywhere = pl.BlockSpec(memory_space=pl.ANY)
@@ -717,16 +736,16 @@
         + working(rows, 16)
         + working(8, 8)
         + [
-            VMEM((MOVE, PIECES) + tile, BF16),
+            VMEM((MOVE, PIECES) + rows_of, BF16),
             VMEM((MOVE,) + tile, F32),
             VMEM((MOVE,) + tile, BF16),
+            VMEM((GROUPS,) + rows_of, BF16),
+            VMEM((GROUPS,) + rows_of, BF16),
+            VMEM((GROUPS,) + rows_of, BF16),
             VMEM((GROUPS,) + tile, BF16),
+            VMEM((MOVE, GROUPS) + rows_of, BF16),
             VMEM((GROUPS,) + tile, BF16),
-            VMEM((GROUPS,) + tile, BF16),
-            VMEM((GROUPS,) + tile, BF16),
-            VMEM((MOVE, GROUPS) + tile, BF16),
-            VMEM((GROUPS,) + tile, BF16),
-            VMEM((MOVE, PIECES) + tile, BF16),
+            VMEM((MOVE, PIECES) + rows_of, BF16),
             VMEM((MOVE,) + tile, BF16),
             dma((MOVE, PIECES)), dma((MOVE, GROUPS)), dma((MOVE,)), dma((GROUPS,)),
             dma((MOVE, GROUPS)), dma((MOVE, PIECES)), dma((GROUPS,)), dma((MOVE,)),

time: 66.2 us -> 69.2 us (1.045)
  Pallas kernels: 65.3 us -> 68.4 us
    pallas_call x1, Pallas kernels: 61.9 us -> 65 us  [decode(): pl.pallas_call(decode_kernel, out_shape=(jax.ShapeDtypeStruct((rows + MOV...]
where the time goes in v3:
time: 69.2 us; the launch traced here: 69 us
  Pallas kernels  68.4 us (99%)
    pallas_call x1, Pallas kernels, decode(): pl.pallas_call(decode_kernel, out_shape=(jax.ShapeDtypeStruct((rows + MOV...  65 us
    pallas_call x1, Pallas kernels, place(): pl.pallas_call(place_kernel, out_shape=(jax.ShapeDtypeStruct(hidden, BF16...  3.41 us

profile of v3, /device:TPU:1, one launch (start us, length us, event | category | flops | bytes accessed | tf_op | source)
XLA Modules:
  0.0 69.0 jit_solution(4008732538856342451)
XLA Ops:
  0.6 65.0 %decode.1 = (f32[15,2,128,128]{3,2,1,0:T(8,128)}, bf16[8,48,256]{2,1,0:T(8,128)(2,1)}, bf16[8,16,256]{2,1,0:T(8,128)(2,1)}) custom-call(s32[1,3]{1,0:T(1,128)} %slots.3, s32[3,32]{1,0:T(4,128)} %bitcast.10, f32[2]{0:T(128)} %decay_log.1, f32[2]{0:T(128)} %time_bias.1, f32[12,2,128,128]{3,2,1,0:T(8,128)} %state_in.1, f32[12,3,1,512]{3,2,1,0:T(1,128)} %bitcast.8, ...), custom_call_target="tpu_custom_call" | custom-call | tf_op jit(solution)/shard_map/decode/pallas_call | solution.py:724
  65.6 3.4 %place.1 = (bf16[12,4,2048]{2,1,0:T(4,128)(2,1)}, f32[12,2,128,128]{3,2,1,0:T(8,128)}, f32[12,3,1,512]{3,2,1,0:T(1,128)}) custom-call(s32[1,3]{1,0:T(1,128)} %slots.3, f32[15,2,128,128]{3,2,1,0:T(8,128)} %get-tuple-element.9.states, bf16[8,48,256]{2,1,0:T(8,128)(2,1)} %get-tuple-element.10.hidden_all, bf16[8,16,256]{2,1,0:T(8,128)(2,1)} %get-tuple-element.11.hidden_moved, ...), custom_call_target="tpu_custom_call" | custom-call | tf_op jit(solution)/shard_map/place/pallas_call | solution.py:810

commit v4 on v2

--- a/solution.py
+++ b/solution.py
@@ -1,3 +1,5 @@
+import functools
+
 import jax
 import jax.numpy as jnp
 from jax import lax
@@ -14,8 +16,24 @@
 HEAD, TAPS, STEPS = 128, 4, 4
 
 
-def piece_holder(piece, core):
-    return 2 * piece + lax.rem(core + piece // 4, 2)
+def member(half, number):
+    return number // 4 * 8 + half * 4 + lax.rem(number, 4)
+
+
+def number_of(group):
+    return group // 8 * 4 + lax.rem(group, 4)
+
+
+def ordered(partner):
+    crossing = [lax.rem(partner[j, 0] // 4, 2) for j in range(MOVE)]
+    count = crossing[0] + crossing[1] + crossing[2]
+    before = [0, crossing[0], crossing[0] + crossing[1]]
+    places = [
+        jnp.where(crossing[j] == 1, before[j], count + j - before[j]) for j in range(MOVE)
+    ]
+    return [
+        sum(jnp.where(places[j] == at, j, 0) for j in range(MOVE)) for at in range(MOVE)
+    ]
 
 
 def split16(value):
@@ -311,7 +329,7 @@
 
 
 def decode_kernel(
-    slots, partner, decay_log, time_bias,
+    crossing, slots, partner, decay_log, time_bias,
     state_in, conv_in, mixed_in, gates_in, zgate_in, weight_in, gain_in, out_weight_in,
     states_out, hidden_all, hidden_moved,
     states, moved, store_sems, conv, mixed, gates, zgate, weight, gain, out_weight, load_sems,
@@ -325,8 +343,13 @@
     me = lax.axis_index("req")
     core = lax.rem(tp, 2)
     place = (tp // 4, lax.rem(tp // 2, 2), core)
-    mine = me // 2
-    holder = piece_holder(mine, core) == me
+    half, mine = lax.rem(me // 4, 2), number_of(me)
+    order = ordered(partner)
+    slot = [slots[0, order[j]] for j in range(MOVE)]
+    streams = list(range(crossing, MOVE)) + list(range(crossing))
+
+    def first_half(j):
+        return 1 - half if j < crossing else half
     held = (held_0, held_1, held_2)
 
     loads = [
@@ -347,8 +370,7 @@
     barrier = pltpu.get_barrier_semaphore()
 
     def greet(k, carry):
-        z, y = lax.rem(7 - lax.rem(me, 8) + k // 4, 8), lax.rem(me // 8 + 2 + k, 4)
-        peer = y * 8 + z
+        peer = member(lax.rem(half + 1 + k // PIECES, 2), lax.rem(mine + k, PIECES))
 
         @pl.when(peer != me)
         def _():
@@ -359,7 +381,7 @@
     tp_peers = movers.peers()
     for peer in tp_peers:
         pl.semaphore_signal(barrier, inc=1, device_id={"tp": peer}, device_id_type=MESH)
-    lax.fori_loop(0, GROUPS, greet, 0)
+    lax.fori_loop(0 if crossing else PIECES, GROUPS, greet, 0)
 
     loads[0].wait()
     conv_rows[...] = jnp.zeros_like(conv_rows)
@@ -367,7 +389,7 @@
         for tap in range(3):
             for part in range(4):
                 conv_rows[j, pl.ds(tap * 4 + part, 1), :] = conv[
-                    slots[0, j], tap, :, part * LANES : (part + 1) * LANES
+                    slot[j], tap, :, part * LANES : (part + 1) * LANES
                 ]
         conv_out[j] = conv_rows[j].astype(BF16)
     loads[1].wait()
@@ -375,7 +397,7 @@
     def pack(piece, carry):
         start = pl.multiple_of(lax.rem(piece, 8) * TILE, TILE)
         for j in range(MOVE):
-            rows_out[j, piece] = states[slots[0, j], piece // 8, pl.ds(start, TILE), :].astype(BF16)
+            rows_out[j, piece] = states[slot[j], piece // 8, pl.ds(start, TILE), :].astype(BF16)
         return carry
 
     lax.fori_loop(0, PIECES, pack, 0)
@@ -436,7 +458,7 @@
         at_out = lax.broadcasted_iota(jnp.int32, target, 0)
         result = jnp.zeros(target, F32)
         for j in range(MOVE):
-            row = jnp.sum(jnp.where(at_row == slots[0, j], value, 0.0), axis=0, keepdims=True)
+            row = jnp.sum(jnp.where(at_row == slot[j], value, 0.0), axis=0, keepdims=True)
             result = jnp.where(at_out == j, jnp.broadcast_to(row, target), result)
         return result
 
@@ -445,22 +467,22 @@
     betas_m = [picked(value) for value in betas]
     zs_m = [picked(value) for value in zs]
 
-    pl.semaphore_wait(barrier, GROUPS - 1 + len(tp_peers))
+    pl.semaphore_wait(barrier, (GROUPS if crossing else PIECES) - 1 + len(tp_peers))
 
     def first(j, piece, peer):
         return pltpu.make_async_remote_copy(
-            src_ref=rows_out.at[j, piece], dst_ref=held[j].at[me], send_sem=send1.at[j, piece],
-            recv_sem=recv1.at[j, me], device_id={"req": peer}, device_id_type=MESH,
+            src_ref=rows_out.at[j, piece], dst_ref=held[j].at[mine], send_sem=send1.at[j, piece],
+            recv_sem=recv1.at[j, mine], device_id={"req": peer}, device_id_type=MESH,
         )
 
     def conv_first(j, peer):
         return pltpu.make_async_remote_copy(
-            src_ref=conv_out.at[j], dst_ref=conv_held.at[me], send_sem=csend1.at[j],
-            recv_sem=crecv1.at[me], device_id={"req": peer}, device_id_type=MESH,
+            src_ref=conv_out.at[j], dst_ref=conv_held.at[mine], send_sem=csend1.at[j],
+            recv_sem=crecv1.at[mine], device_id={"req": peer}, device_id_type=MESH,
         )
 
     for j in range(MOVE):
-        peer = piece_holder(CONV_PIECE[j], core)
+        peer = member(first_half(j), CONV_PIECE[j])
 
         @pl.when(peer != me)
         def _():
@@ -468,13 +490,13 @@
 
         @pl.when(peer == me)
         def _():
-            conv_held[me] = conv_out[j]
+            conv_held[mine] = conv_out[j]
 
     for j in range(MOVE):
 
         def send_piece(k, carry):
             piece = lax.rem(mine + k, PIECES)
-            peer = piece_holder(piece, core)
+            peer = member(first_half(j), piece)
 
             @pl.when(peer != me)
             def _():
@@ -482,7 +504,7 @@
 
             @pl.when(peer == me)
             def _():
-                held[j][me] = rows_out[j, piece]
+                held[j][mine] = rows_out[j, piece]
 
             return carry
 
@@ -507,78 +529,86 @@
     stores[0].start()
     everyone.along_x()
 
-    def second(j, dest):
+    def second(j, number):
         return pltpu.make_async_remote_copy(
-            src_ref=turned.at[j, dest], dst_ref=landed.at[j, mine], send_sem=send2.at[j, dest],
-            recv_sem=recv2.at[j, mine], device_id={"req": dest}, device_id_type=MESH,
-        )
-
-    def conv_second(j, dest):
+            src_ref=turned.at[j, number], dst_ref=landed.at[j, mine], send_sem=send2.at[j, number],
+            recv_sem=recv2.at[j, mine], device_id={"req": member(half, number)}, device_id_type=MESH,
+        )
+
+    def conv_second(j, number):
         return pltpu.make_async_remote_copy(
-            src_ref=conv_turned.at[dest], dst_ref=conv_landed.at[j], send_sem=csend2.at[dest],
-            recv_sem=crecv2.at[j], device_id={"req": dest}, device_id_type=MESH,
-        )
-
-    for j in range(MOVE):
-
-        @pl.when(holder)
+            src_ref=conv_turned.at[number], dst_ref=conv_landed.at[j], send_sem=csend2.at[number],
+            recv_sem=crecv2.at[j], device_id={"req": member(half, number)}, device_id_type=MESH,
+        )
+
+    for j in streams:
+
+        def wait_first(k, carry):
+            number = lax.rem(mine + k, PIECES)
+            source = member(first_half(j), number)
+
+            @pl.when(source != me)
+            def _():
+                pltpu.make_async_remote_copy(
+                    src_ref=rows_out.at[j, 0], dst_ref=held[j].at[number], send_sem=send1.at[j, 0],
+                    recv_sem=recv1.at[j, number], device_id={"req": source}, device_id_type=MESH,
+                ).wait_recv()
+
+            return carry
+
+        lax.fori_loop(0, PIECES, wait_first, 0)
+
+        def turn(k, carry):
+            number = lax.rem(mine + k, PIECES)
+            source = partner[order[j], member(half, number)]
+            turned[j, number] = held[j][number_of(source)]
+
+            @pl.when(k > 0)
+            def _():
+                second(j, number).start()
+
+            return carry
+
+        lax.fori_loop(0, PIECES, turn, 0)
+        landed[j, mine] = turned[j, mine]
+
+        @pl.when(mine == CONV_PIECE[j])
         def _():
-            def wait_first(k, carry):
-                group = lax.rem(me + k, GROUPS)
-                pltpu.make_async_remote_copy(
-                    src_ref=rows_out.at[j, 0], dst_ref=held[j].at[group], send_sem=send1.at[j, 0],
-                    recv_sem=recv1.at[j, group], device_id={"req": group}, device_id_type=MESH,
-                ).wait_recv()
+            def wait_conv(k, carry):
+                number = lax.rem(mine + k, PIECES)
+                source = member(first_half(j), number)
+
+                @pl.when(source != me)
+                def _():
+                    pltpu.make_async_remote_copy(
+                        src_ref=conv_out.at[0], dst_ref=conv_held.at[number], send_sem=csend1.at[0],
+                        recv_sem=crecv1.at[number], device_id={"req": source}, device_id_type=MESH,
+                    ).wait_recv()
+
                 return carry
 
-            lax.fori_loop(1, GROUPS, wait_first, 0)
-
-            def turn(k, carry):
-                dest = lax.rem(me + k, GROUPS)
-                turned[j, dest] = held[j][partner[j, dest]]
+            lax.fori_loop(0, PIECES, wait_conv, 0)
+
+            def turn_conv(k, carry):
+                number = lax.rem(mine + k, PIECES)
+                source = partner[order[j], member(half, number)]
+                conv_turned[number] = conv_held[number_of(source)]
 
                 @pl.when(k > 0)
                 def _():
-                    second(j, dest).start()
+                    conv_second(j, number).start()
 
                 return carry
 
-            lax.fori_loop(0, GROUPS, turn, 0)
-            landed[j, mine] = turned[j, me]
-
-        @pl.when(jnp.logical_and(holder, mine == CONV_PIECE[j]))
+            lax.fori_loop(0, PIECES, turn_conv, 0)
+            conv_landed[j] = conv_turned[mine]
+
+    everyone.along_z()
+
+    for j in range(MOVE):
+        @pl.when(mine != CONV_PIECE[j])
         def _():
-            def wait_conv(k, carry):
-                group = lax.rem(me + k, GROUPS)
-                pltpu.make_async_remote_copy(
-                    src_ref=conv_out.at[0], dst_ref=conv_held.at[group], send_sem=csend1.at[0],
-                    recv_sem=crecv1.at[group], device_id={"req": group}, device_id_type=MESH,
-                ).wait_recv()
-                return carry
-
-            lax.fori_loop(1, GROUPS, wait_conv, 0)
-
-            def turn_conv(k, carry):
-                dest = lax.rem(me + k, GROUPS)
-                conv_turned[dest] = conv_held[partner[j, dest]]
-
-                @pl.when(k > 0)
-                def _():
-                    conv_second(j, dest).start()
-
-                return carry
-
-            lax.fori_loop(0, GROUPS, turn_conv, 0)
-            conv_landed[j] = conv_turned[me]
-
-    everyone.along_z()
-
-    for j in range(MOVE):
-        source = piece_holder(CONV_PIECE[j], core)
-
-        @pl.when(source != me)
-        def _():
-            conv_second(j, source).wait_recv()
+            conv_second(j, CONV_PIECE[j]).wait_recv()
 
     at_out = lax.broadcasted_iota(jnp.int32, (8, LANES), 0)
     window_m = []
@@ -599,21 +629,18 @@
     read_side(left_m, queries, keys)
     gram = products(queries, keys)
 
-    for j in range(MOVE):
-
-        def wait_second(piece, carry):
-            source = piece_holder(piece, core)
-
-            @pl.when(source != me)
-            def _():
-                pltpu.make_async_remote_copy(
-                    src_ref=turned.at[j, 0], dst_ref=landed.at[j, piece], send_sem=send2.at[j, 0],
-                    recv_sem=recv2.at[j, piece], device_id={"req": source}, device_id_type=MESH,
-                ).wait_recv()
-
+    for j in streams:
+
+        def wait_second(k, carry):
+            piece = lax.rem(mine + k, PIECES)
+            pltpu.make_async_remote_copy(
+                src_ref=turned.at[j, 0], dst_ref=landed.at[j, piece], send_sem=send2.at[j, 0],
+                recv_sem=recv2.at[j, piece], device_id={"req": member(half, piece)},
+                device_id_type=MESH,
+            ).wait_recv()
             return carry
 
-        lax.fori_loop(0, PIECES, wait_second, 0)
+        lax.fori_loop(1, PIECES, wait_second, 0)
         lhs = left_m[:, j, :].astype(BF16)
         for h in range(2):
             block = landed[j, h * 8 : (h + 1) * 8].reshape(HEAD, HEAD)
@@ -636,41 +663,37 @@
     stores[2].start()
     everyone.back_core()
 
-    def done_first(piece, carry):
-        peer = piece_holder(piece, core)
-
-        @pl.when(peer != me)
-        def _():
-            for j in range(MOVE):
+    for j in range(MOVE):
+
+        def done_first(piece, carry):
+            peer = member(first_half(j), piece)
+
+            @pl.when(peer != me)
+            def _():
                 first(j, piece, peer).wait_send()
 
-        return carry
-
-    lax.fori_loop(0, PIECES, done_first, 0)
-    for j in range(MOVE):
-        peer = piece_holder(CONV_PIECE[j], core)
+            return carry
+
+        lax.fori_loop(0, PIECES, done_first, 0)
+        peer = member(first_half(j), CONV_PIECE[j])
 
         @pl.when(peer != me)
         def _():
             conv_first(j, peer).wait_send()
 
-    @pl.when(holder)
-    def _():
         def done_second(k, carry):
-            for j in range(MOVE):
-                second(j, lax.rem(me + k, GROUPS)).wait_send()
+            second(j, lax.rem(mine + k, PIECES)).wait_send()
             return carry
 
-        lax.fori_loop(1, GROUPS, done_second, 0)
-        for j in range(MOVE):
-
-            @pl.when(mine == CONV_PIECE[j])
-            def _():
-                def done_conv(k, carry):
-                    conv_second(j, lax.rem(me + k, GROUPS)).wait_send()
-                    return carry
-
-                lax.fori_loop(1, GROUPS, done_conv, 0)
+        lax.fori_loop(1, PIECES, done_second, 0)
+
+        @pl.when(mine == CONV_PIECE[j])
+        def _():
+            def done_conv(k, carry):
+                conv_second(j, lax.rem(mine + k, PIECES)).wait_send()
+                return carry
+
+            lax.fori_loop(1, PIECES, done_conv, 0)
 
     everyone.end()
     stores[1].start()
@@ -684,7 +707,7 @@
 
 
 def decode(
-    slots, partner, decay_log, time_bias, state, conv, mixed, gates, zgate, weight, gain, out_weight
+    crossing, slots, partner, decay_log, time_bias, state, conv, mixed, gates, zgate, weight, gain, out_weight
 ):
     rows = state.shape[0]
     width = out_weight.shape[1] // 8
@@ -703,7 +726,7 @@
         ]
 
     return pl.pallas_call(
-        decode_kernel,
+        functools.partial(decode_kernel, crossing),
         out_shape=(
             jax.ShapeDtypeStruct((rows + MOVE,) + state.shape[1:], F32),
             jax.ShapeDtypeStruct((8, rows * STEPS, width), BF16),
@@ -720,54 +743,58 @@
             VMEM((MOVE, PIECES) + tile, BF16),
             VMEM((MOVE,) + tile, F32),
             VMEM((MOVE,) + tile, BF16),
-            VMEM((GROUPS,) + tile, BF16),
-            VMEM((GROUPS,) + tile, BF16),
-            VMEM((GROUPS,) + tile, BF16),
-            VMEM((GROUPS,) + tile, BF16),
-            VMEM((MOVE, GROUPS) + tile, BF16),
-            VMEM((GROUPS,) + tile, BF16),
+            VMEM((PIECES,) + tile, BF16),
+            VMEM((PIECES,) + tile, BF16),
+            VMEM((PIECES,) + tile, BF16),
+            VMEM((PIECES,) + tile, BF16),
+            VMEM((MOVE, PIECES) + tile, BF16),
+            VMEM((PIECES,) + tile, BF16),
             VMEM((MOVE, PIECES) + tile, BF16),
             VMEM((MOVE,) + tile, BF16),
-            dma((MOVE, PIECES)), dma((MOVE, GROUPS)), dma((MOVE,)), dma((GROUPS,)),
-            dma((MOVE, GROUPS)), dma((MOVE, PIECES)), dma((GROUPS,)), dma((MOVE,)),
+            dma((MOVE, PIECES)), dma((MOVE, PIECES)), dma((MOVE,)), dma((PIECES,)),
+            dma((MOVE, PIECES)), dma((MOVE, PIECES)), dma((PIECES,)), dma((MOVE,)),
         ]
         + Reduction.scratch(rows * STEPS, width)
         + ShortReduction.scratch(TILE, width),
         compiler_params=pltpu.CompilerParams(
-            collective_id=0, has_side_effects=True, vmem_limit_bytes=58 << 20
+            collective_id=crossing, has_side_effects=True, vmem_limit_bytes=58 << 20
         ),
         name="decode",
     )(slots, partner, decay_log, time_bias, *arrays)
 
 
 def place_kernel(
-    slots, states, hidden_all, hidden_moved, mixed, hidden, new_state, new_conv,
+    slots, partner, states, hidden_all, hidden_moved, mixed, hidden, new_state, new_conv,
     held, kept, changed, latest, fresh, out, load_sems, store_sems,
 ):
     rows = mixed.shape[0]
     width = hidden_all.shape[2]
+    slot = [slots[0, at] for at in ordered(partner)]
     loads, stores = [], []
     for r in range(rows):
         source = r
         for j in range(MOVE):
-            source = jnp.where(slots[0, j] == r, rows + j, source)
+            source = jnp.where(slot[j] == r, rows + j, source)
         loads.append(pltpu.make_async_copy(states.at[source], held.at[r], load_sems.at[r]))
         stores.append(pltpu.make_async_copy(held.at[r], new_state.at[r], store_sems.at[r]))
     for at, (src, dst) in enumerate(((hidden_all, kept), (hidden_moved, changed), (mixed, latest))):
         loads.append(pltpu.make_async_copy(src, dst, load_sems.at[rows + at]))
-    stores.append(pltpu.make_async_copy(out, hidden, store_sems.at[rows]))
-    stores.append(pltpu.make_async_copy(fresh, new_conv, store_sems.at[rows + 1]))
+    stores.append(pltpu.make_async_copy(fresh, new_conv, store_sems.at[rows]))
+    for block in range(8):
+        cut = pl.ds(block * width, width)
+        stores.append(
+            pltpu.make_async_copy(
+                out.at[:, :, cut], hidden.at[:, :, cut], store_sems.at[rows + 1 + block]
+            )
+        )
     for load in loads[rows:] + loads[:rows]:
         load.start()
-    for r in range(rows):
-        loads[r].wait()
-        stores[r].start()
     for load in loads[rows:]:
         load.wait()
     values = latest[...].astype(F32)
     for tap in range(3):
         fresh[:, tap, 0, :] = values[:, tap + 1, :]
-    stores[rows + 1].start()
+    stores[rows].start()
     for block in range(8):
         cut = slice(block * width, (block + 1) * width)
         stay = kept[block].astype(F32)
@@ -775,14 +802,17 @@
         for r in range(rows):
             value = stay[r * STEPS : (r + 1) * STEPS, :]
             for j in range(MOVE):
-                value = jnp.where(slots[0, j] == r, came[j * STEPS : (j + 1) * STEPS, :], value)
+                value = jnp.where(slot[j] == r, came[j * STEPS : (j + 1) * STEPS, :], value)
             out[r, :, cut] = value.astype(BF16)
-    stores[rows].start()
+        stores[rows + 1 + block].start()
+        for r in range(rows * block // 8, rows * (block + 1) // 8):
+            loads[r].wait()
+            stores[r].start()
     for store in stores:
         store.wait()
 
 
-def place(slots, states, hidden_all, hidden_moved, mixed):
+def place(slots, partner, states, hidden_all, hidden_moved, mixed):
     rows = mixed.shape[0]
     dma = pltpu.SemaphoreType.DMA
     anywhere = pl.BlockSpec(memory_space=pl.ANY)
@@ -795,16 +825,16 @@
             jax.ShapeDtypeStruct((rows,) + states.shape[1:], F32),
             jax.ShapeDtypeStruct(conv, F32),
         ),
-        in_specs=[pl.BlockSpec(memory_space=pltpu.SMEM)] + [anywhere] * 4,
+        in_specs=[pl.BlockSpec(memory_space=pltpu.SMEM)] * 2 + [anywhere] * 4,
         out_specs=(anywhere,) * 3,
         scratch_shapes=[
             VMEM((rows,) + states.shape[1:], F32), VMEM(hidden_all.shape, BF16),
             VMEM(hidden_moved.shape, BF16), VMEM(mixed.shape, BF16), VMEM(conv, F32),
-            VMEM(hidden, BF16), dma((rows + 3,)), dma((rows + 2,)),
+            VMEM(hidden, BF16), dma((rows + 3,)), dma((rows + 9,)),
         ],
         compiler_params=pltpu.CompilerParams(vmem_limit_bytes=58 << 20),
         name="place",
-    )(slots, states, hidden_all, hidden_moved, mixed)
+    )(slots, partner, states, hidden_all, hidden_moved, mixed)
 
 
 def per_device(
@@ -822,12 +852,17 @@
     moved_slots,
 ):
     fresh = mixed.reshape(mixed.shape[0], mixed.shape[1], mixed.shape[3])
-    states, hidden_all, hidden_moved = decode(
-        moved_slots, partner.T, decay_log, time_bias, state, conv_state.transpose(0, 2, 1, 3),
+    masks = partner.T
+    states, hidden_all, hidden_moved = lax.switch(
+        jnp.sum(lax.rem(partner[0] // 4, 2)),
+        [functools.partial(decode, crossing) for crossing in range(MOVE + 1)],
+        moved_slots, masks, decay_log, time_bias, state, conv_state.transpose(0, 2, 1, 3),
         fresh, gates.transpose(1, 2, 3, 0), output_gate, conv_weight, norm_gain.reshape(1, -1),
         out_weight,
     )
-    hidden, new_state, new_conv = place(moved_slots, states, hidden_all, hidden_moved, fresh)
+    hidden, new_state, new_conv = place(
+        moved_slots, masks, states, hidden_all, hidden_moved, fresh
+    )
     return (hidden, new_state, new_conv.transpose(0, 2, 1, 3))
 
 

time: 66.2 us -> 65.4 us (0.988)
  Pallas kernels: 65.3 us -> 61.8 us
  between operations: 0.64 us -> 1.47 us
  local copies, waits for them, and re-layouts: 0 us -> 0.8 us
    pallas_call x1, Pallas kernels: 61.9 us -> 57.1 us  [decode(): pl.pallas_call(functools.partial(decode_kernel, crossing), out_shape=(jax...]
    pallas_call x1, Pallas kernels: 3.41 us -> 4.71 us  [place(): pl.pallas_call(place_kernel, out_shape=(jax.ShapeDtypeStruct(hidden, BF16...]
    slice x0 -> x1, local copies, waits for them, and re-layouts: none -> 0.8 us  [per_device(): partner[0] // 4]
where the time goes in v4:
time: 65.4 us; the launch traced here: 65.2 us
  Pallas kernels  61.8 us (94%)
  between operations  1.47 us (2%)
  local copies, waits for them, and re-layouts  0.8 us (1%)
    pallas_call x1, Pallas kernels, decode(): pl.pallas_call(functools.partial(decode_kernel, crossing), out_shape=(jax...  57.1 us
    pallas_call x1, Pallas kernels, place(): pl.pallas_call(place_kernel, out_shape=(jax.ShapeDtypeStruct(hidden, BF16...  4.71 us

profile of v4, /device:TPU:1, one launch (start us, length us, event | category | flops | bytes accessed | tf_op | source)
XLA Modules:
  0.0 65.2 jit_solution(10058008613866317169)
XLA Ops:
  0.6 0.8 %slice_reduce_fusion = s32[3]{0:T(128)S(1)} fusion(s32[32,3]{0,1:T(4,128)} %param.26), kind=kLoop, calls=%fused_computation.2 | loop fusion | bytes 24 | tf_op jit(solution)/shard_map/slice | solution.py:857
  1.4 0.6 fusion.1
  2.7 57.6 %conditional.1 = ((f32[15,2,128,128]{3,2,1,0:T(8,128)S(1)}, bf16[8,48,256]{2,1,0:T(8,128)(2,1)S(1)}, bf16[8,16,256]{2,1,0:T(8,128)(2,1)S(1)})) conditional(s32[]{:T(128)} %clamp.3, (s32[1,3]{1,0:T(1,128)}, s32[3,32]{1,0:T(4,128)}, f32[2]{0:T(128)}, f32[2]{0:T(128)}, f32[12,2,128,128]{3,2,1,0:T(8,128)}, ...), branch_computations={%region_1.2_spmd, %region_2.3_spmd, %region_3.4_spmd, %region_4.5_... | conditional | bytes 8 | solution.py:856
  2.8 57.1 %decode.6 = (f32[15,2,128,128]{3,2,1,0:T(8,128)S(1)}, bf16[8,48,256]{2,1,0:T(8,128)(2,1)S(1)}, bf16[8,16,256]{2,1,0:T(8,128)(2,1)S(1)}) custom-call(s32[1,3]{1,0:T(1,128)} %get-tuple-element.120.slots, s32[3,32]{1,0:T(4,128)} %get-tuple-element.121.partner, f32[2]{0:T(128)} %get-tuple-element.122.decay_log, f32[2]{0:T(128)} %get-tuple-element.123.time_bias, ...), custom_call_target="tpu_custom_call" | custom-call | tf_op jit(solution)/shard_map/cond/branch_2_fun/decode/pallas_call | solution.py:728
  60.3 4.7 %place.1 = (bf16[12,4,2048]{2,1,0:T(4,128)(2,1)}, f32[12,2,128,128]{3,2,1,0:T(8,128)}, f32[12,3,1,512]{3,2,1,0:T(1,128)}) custom-call(s32[1,3]{1,0:T(1,128)} %slots.1, s32[3,32]{1,0:T(4,128)} %bitcast.23, f32[15,2,128,128]{3,2,1,0:T(8,128)S(1)} %get-tuple-element.153.states, bf16[8,48,256]{2,1,0:T(8,128)(2,1)S(1)} %get-tuple-element.154.hidden_all, ...), custom_call_target="tpu_custom_call" | custom-call | tf_op jit(solution)/shard_map/place/pallas_call | solution.py:821

commit v5 on v4

--- a/solution.py
+++ b/solution.py
@@ -765,20 +765,20 @@
 
 def place_kernel(
     slots, partner, states, hidden_all, hidden_moved, mixed, hidden, new_state, new_conv,
-    held, kept, changed, latest, fresh, out, load_sems, store_sems,
+    latest, fresh, out, load_sem, store_sems,
 ):
     rows = mixed.shape[0]
     width = hidden_all.shape[2]
     slot = [slots[0, at] for at in ordered(partner)]
-    loads, stores = [], []
+    load = pltpu.make_async_copy(mixed, latest, load_sem)
+    load.start()
+    stores = []
     for r in range(rows):
         source = r
         for j in range(MOVE):
             source = jnp.where(slot[j] == r, rows + j, source)
-        loads.append(pltpu.make_async_copy(states.at[source], held.at[r], load_sems.at[r]))
-        stores.append(pltpu.make_async_copy(held.at[r], new_state.at[r], store_sems.at[r]))
-    for at, (src, dst) in enumerate(((hidden_all, kept), (hidden_moved, changed), (mixed, latest))):
-        loads.append(pltpu.make_async_copy(src, dst, load_sems.at[rows + at]))
+        stores.append(pltpu.make_async_copy(states.at[source], new_state.at[r], store_sems.at[r]))
+        stores[r].start()
     stores.append(pltpu.make_async_copy(fresh, new_conv, store_sems.at[rows]))
     for block in range(8):
         cut = pl.ds(block * width, width)
@@ -787,27 +787,21 @@
                 out.at[:, :, cut], hidden.at[:, :, cut], store_sems.at[rows + 1 + block]
             )
         )
-    for load in loads[rows:] + loads[:rows]:
-        load.start()
-    for load in loads[rows:]:
-        load.wait()
-    values = latest[...].astype(F32)
-    for tap in range(3):
-        fresh[:, tap, 0, :] = values[:, tap + 1, :]
-    stores[rows].start()
     for block in range(8):
         cut = slice(block * width, (block + 1) * width)
-        stay = kept[block].astype(F32)
-        came = changed[block].astype(F32)
+        stay = hidden_all[block].astype(F32)
+        came = hidden_moved[block].astype(F32)
         for r in range(rows):
             value = stay[r * STEPS : (r + 1) * STEPS, :]
             for j in range(MOVE):
                 value = jnp.where(slot[j] == r, came[j * STEPS : (j + 1) * STEPS, :], value)
             out[r, :, cut] = value.astype(BF16)
         stores[rows + 1 + block].start()
-        for r in range(rows * block // 8, rows * (block + 1) // 8):
-            loads[r].wait()
-            stores[r].start()
+    load.wait()
+    values = latest[...].astype(F32)
+    for tap in range(3):
+        fresh[:, tap, 0, :] = values[:, tap + 1, :]
+    stores[rows].start()
     for store in stores:
         store.wait()
 
@@ -816,6 +810,7 @@
     rows = mixed.shape[0]
     dma = pltpu.SemaphoreType.DMA
     anywhere = pl.BlockSpec(memory_space=pl.ANY)
+    vmem = pl.BlockSpec(memory_space=VMEM)
     hidden = (rows, STEPS, 8 * hidden_all.shape[2])
     conv = (rows, TAPS - 1, 1, mixed.shape[2])
     return pl.pallas_call(
@@ -825,14 +820,12 @@
             jax.ShapeDtypeStruct((rows,) + states.shape[1:], F32),
             jax.ShapeDtypeStruct(conv, F32),
         ),
-        in_specs=[pl.BlockSpec(memory_space=pltpu.SMEM)] * 2 + [anywhere] * 4,
+        in_specs=[pl.BlockSpec(memory_space=pltpu.SMEM)] * 2 + [vmem] * 3 + [anywhere],
         out_specs=(anywhere,) * 3,
         scratch_shapes=[
-            VMEM((rows,) + states.shape[1:], F32), VMEM(hidden_all.shape, BF16),
-            VMEM(hidden_moved.shape, BF16), VMEM(mixed.shape, BF16), VMEM(conv, F32),
-            VMEM(hidden, BF16), dma((rows + 3,)), dma((rows + 9,)),
+            VMEM(mixed.shape, BF16), VMEM(conv, F32), VMEM(hidden, BF16), dma, dma((rows + 9,)),
         ],
-        compiler_params=pltpu.CompilerParams(vmem_limit_bytes=58 << 20),
+        compiler_params=pltpu.CompilerParams(vmem_limit_bytes=40 << 20),
         name="place",
     )(slots, partner, states, hidden_all, hidden_moved, mixed)
 

time: 65.4 us -> 63.3 us (0.968)
  Pallas kernels: 61.8 us -> 59.7 us
    pallas_call x1, Pallas kernels: 4.71 us -> 2.53 us  [place(): pl.pallas_call(place_kernel, out_shape=(jax.ShapeDtypeStruct(hidden, BF16...]
where the time goes in v5:
time: 63.3 us; the launch traced here: 63 us
  Pallas kernels  59.7 us (94%)
  between operations  1.47 us (2%)
  local copies, waits for them, and re-layouts  0.8 us (1%)
  other arithmetic  0.65 us (1%)
    pallas_call x1, Pallas kernels, decode(): pl.pallas_call(functools.partial(decode_kernel, crossing), out_shape=(jax...  57.1 us
    pallas_call x1, Pallas kernels, place(): pl.pallas_call(place_kernel, out_shape=(jax.ShapeDtypeStruct(hidden, BF16...  2.53 us

profile of v5, /device:TPU:1, one launch (start us, length us, event | category | flops | bytes accessed | tf_op | source)
XLA Modules:
  0.0 63.0 jit_solution(10938760717057972280)
XLA Ops:
  0.6 0.8 %slice_reduce_fusion = s32[3]{0:T(128)S(1)} fusion(s32[32,3]{0,1:T(4,128)} %param.26), kind=kLoop, calls=%fused_computation.2 | loop fusion | bytes 24 | tf_op jit(solution)/shard_map/slice | solution.py:850
  1.4 0.6 %fusion.1 = s32[]{:T(128)} fusion(s32[3]{0:T(128)S(1)} %slice_reduce_fusion), kind=kLoop, calls=%fused_computation.8 | loop fusion | flops 65 | bytes 16 | tf_op jit(solution)/shard_map/reduce_sum | solution.py:850
  2.7 57.6 %conditional.1 = ((f32[15,2,128,128]{3,2,1,0:T(8,128)S(1)}, bf16[8,48,256]{2,1,0:T(8,128)(2,1)S(1)}, bf16[8,16,256]{2,1,0:T(8,128)(2,1)S(1)})) conditional(s32[]{:T(128)} %clamp.3, (s32[1,3]{1,0:T(1,128)}, s32[3,32]{1,0:T(4,128)}, f32[2]{0:T(128)}, f32[2]{0:T(128)}, f32[12,2,128,128]{3,2,1,0:T(8,128)}, ...), branch_computations={%region_1.2_spmd, %region_2.3_spmd, %region_3.4_spmd, %region_4.5_... | conditional | bytes 8 | solution.py:849
  2.8 57.1 %decode.6 = (f32[15,2,128,128]{3,2,1,0:T(8,128)S(1)}, bf16[8,48,256]{2,1,0:T(8,128)(2,1)S(1)}, bf16[8,16,256]{2,1,0:T(8,128)(2,1)S(1)}) custom-call(s32[1,3]{1,0:T(1,128)} %get-tuple-element.120.slots, s32[3,32]{1,0:T(4,128)} %get-tuple-element.121.partner, f32[2]{0:T(128)} %get-tuple-element.122.decay_log, f32[2]{0:T(128)} %get-tuple-element.123.time_bias, ...), custom_call_target="tpu_custom_call" | custom-call | tf_op jit(solution)/shard_map/cond/branch_2_fun/decode/pallas_call | solution.py:728
  60.3 2.5 %place.1 = (bf16[12,4,2048]{2,1,0:T(4,128)(2,1)}, f32[12,2,128,128]{3,2,1,0:T(8,128)}, f32[12,3,1,512]{3,2,1,0:T(1,128)}) custom-call(s32[1,3]{1,0:T(1,128)} %slots.1, s32[3,32]{1,0:T(4,128)} %bitcast.23, f32[15,2,128,128]{3,2,1,0:T(8,128)S(1)} %get-tuple-element.153.states, bf16[8,48,256]{2,1,0:T(8,128)(2,1)S(1)} %get-tuple-element.154.hidden_all, ...), custom_call_target="tpu_custom_call" | custom-call | tf_op jit(solution)/shard_map/place/pallas_call | solution.py:816
